TPU v7x, 256 devices: a whole 4x4x8 slice. The times are simulated.
256 devices in a mesh: sub: 8 (over x_hi, y), sens: 2 (over core), cell: 16 (over x_lo, z).
Axes of the slice: x: 4 (x_hi: 2, x_lo: 2; x = x_hi * 2 + x_lo), y: 4, z: 8, core: 2. Of those that a mesh axis runs over, the one named last changes fastest.
Arguments:
- snapshots: bfloat16 [8, 4, 2, 64, 1024], P('sub', None, None, 'cell', 'sens'), may hold values from -6 to 6
- sensor_modes: bfloat16 [8, 1024, 256], P('sub', 'sens'), may hold values from -8 to 8
- aperture_curvature: bfloat16 [8, 1024], P('sub', 'sens'), may hold values from 0 to 29952
- depth_offset: bfloat16 [8, 1024], P('sub', 'sens'), may hold values from -60 to 60
- cell_modes: bfloat16 [8, 4, 64, 2, 128, 128], P('sub', None, None, None, 'cell'), may hold values from -6 to 6
- ref_wavenumber: float32 [8, 4], P('sub'), may hold values from 0.3 to 0.7
- range_start: float32 [8], P('sub'), may hold values from 1000 to 3000
- mode_counts: int32 [8, 4], P('sub'), may hold values from 32 to 64, as said below
Outputs:
- ambiguity: float32 [4, 128, 128], P(None, 'cell', ('sub', 'sens'))
Inputs may be any that keep to these rules, and one draw needn't show every extreme that they name: `mode_counts`: mode counts lie between half the table and the whole table; one entry equals 64.
All inputs are finite; a program needn't handle non-finite values.
Results may differ from a plain program's by a relative error of at most 0.0009.
Values may be sent and summed in bfloat16 or wider, within the bound.
No kernel may reach another device: no remote copies, remote signals or barrier semaphores. Data moves between devices by JAX's collectives and lax.ppermute only.
A program may use at most 128 MiB of HBM per device.

v0:
```python
import jax
import jax.numpy as jnp
from jax import lax
from jax.sharding import PartitionSpec as P

range_step = 20.0
depth_step = 2.0
tiny = 1e-06


def replica_block(sensor_rows, curvature, offsets, modal_block, wavenumber, ranges, depths):
    mode_total = modal_block.shape[0]
    summed = jnp.dot(
        sensor_rows, modal_block.reshape(mode_total, -1), preferred_element_type=jnp.float32
    )
    summed = summed.reshape((sensor_rows.shape[0],) + modal_block.shape[1:])
    phase_term = (
        wavenumber
        * (curvature[:, None, None] - offsets[:, None, None] * depths[None, None, :])
        / ranges[None, :, None]
    )
    cosine = jnp.cos(phase_term)
    sine_part = jnp.sin(phase_term)
    real_part = (summed[:, 0] * cosine - summed[:, 1] * sine_part).astype(jnp.bfloat16)
    imag_part = (summed[:, 0] * sine_part + summed[:, 1] * cosine).astype(jnp.bfloat16)
    energy = jnp.sum(
        jnp.square(real_part.astype(jnp.float32)) + jnp.square(imag_part.astype(jnp.float32)),
        axis=0,
    )
    stacked = jnp.concatenate([real_part, imag_part], axis=0).reshape(2 * sensor_rows.shape[0], -1)
    return (stacked, energy)


def beam_rows(signal, stacked):
    real_x = signal[0]
    imag_x = signal[1]
    upper_rows = jnp.concatenate([real_x, imag_x], axis=1)
    lower_rows = jnp.concatenate([imag_x, -real_x], axis=1)
    return jnp.dot(
        jnp.concatenate([upper_rows, lower_rows], axis=0),
        stacked,
        preferred_element_type=jnp.float32,
    )


def local(
    snapshots,
    sensor_modes,
    aperture_curvature,
    depth_offset,
    cell_modes,
    ref_wavenumber,
    range_start,
    mode_counts,
):
    bin_count = cell_modes.shape[1]
    mode_total = cell_modes.shape[2]
    row_total = cell_modes.shape[4]
    depth_total = cell_modes.shape[5]
    row_index = (
        lax.axis_index("cell") * row_total + jnp.arange(row_total, dtype=jnp.int32)
    ).astype(jnp.float32)
    signal, sensor_table, curv_table, offset_table = (
        snapshots,
        sensor_modes,
        aperture_curvature,
        depth_offset,
    )
    depth_index = jnp.arange(depth_total, dtype=jnp.int32)
    depths = depth_step * depth_index.astype(jnp.float32)
    ranges = range_start[0] + range_step * row_index
    curvature = curv_table[0].astype(jnp.float32)
    offsets = offset_table[0].astype(jnp.float32)
    mode_index = jnp.arange(mode_total, dtype=jnp.int32)
    stacked_list = []
    energy_list = []
    for bin_index in range(bin_count):
        kept_modes = (mode_index < mode_counts[0, bin_index]).astype(jnp.bfloat16)
        modal_block = cell_modes[0, bin_index] * kept_modes[:, None, None, None]
        sensor_rows = sensor_table[0, :, bin_index * mode_total : (bin_index + 1) * mode_total]
        stacked, part_energy = replica_block(
            sensor_rows,
            curvature,
            offsets,
            modal_block,
            ref_wavenumber[0, bin_index],
            ranges,
            depths,
        )
        stacked_list.append(stacked)
        energy_list.append(part_energy)
    energy = jnp.stack(energy_list)
    whole_signal = lax.all_gather(signal, "cell", axis=3, tiled=True)
    per_bin = []
    for bin_index in range(bin_count):
        product = beam_rows(whole_signal[0, bin_index], stacked_list[bin_index])
        per_bin.append(product.reshape(2, whole_signal.shape[3], row_total, -1))
    beams = jnp.stack(per_bin)
    beams, energy = (
        lax.psum_scatter(beams, ("sub", "sens"), scatter_dimension=4, tiled=True),
        lax.psum_scatter(energy, ("sub", "sens"), scatter_dimension=2, tiled=True),
    )
    power = jnp.mean(jnp.square(beams[:, 0]) + jnp.square(beams[:, 1]), axis=1)
    return 10.0 * jnp.log10((power + tiny) / (energy + tiny))


def solution(mesh):
    return jax.shard_map(
        local,
        mesh=mesh,
        in_specs=(
            P("sub", None, None, "cell", "sens"),
            P("sub", "sens", None),
            P("sub", "sens"),
            P("sub", "sens"),
            P("sub", None, None, None, "cell", None),
            P("sub", None),
            P("sub"),
            P("sub", None),
        ),
        out_specs=P(None, "cell", ("sub", "sens")),
        check_vma=False,
    )
```

profile of v0, /device:TPU:2, one launch (start us, length us, event | category | flops | bytes accessed | tf_op | source)
XLA Modules:
  0.0 230.9 jit_solution(17684024101272387079)
XLA Ops:
  7.2 1.5 fusion.70
  8.7 0.7 convert_element_type.169
  9.4 0.7 convert_element_type.168
  10.1 1.5 fusion.71
  11.5 1.2 compare_convert_fusion
  12.7 1.3 compare_convert_fusion.2
  14.1 1.5 slice_multiply_fusion
  15.8 2.7 %fusion.52 = f32[2048,512]{1,0:T(8,128)} fusion(bf16[64,2048]{1,0:T(8,128)(2,1)S(1)} %mul.266, bf16[1,512,256]{2,1,0:T(8,128)(2,1)S(1)} %copy-done.4), kind=kOutput, calls=%fused_computation.120 | convolution fusion | flops 134217728 | bytes 4587520 | tf_op jit(solution)/shard_map/dot_general | solution.py:13
  18.5 2.7 %fusion.48 = f32[2048,512]{1,0:T(8,128)} fusion(bf16[64,2048]{1,0:T(8,128)(2,1)S(1)} %mul.291, bf16[1,512,256]{2,1,0:T(8,128)(2,1)S(1)} %copy-done.4), kind=kOutput, calls=%fused_computation.116 | convolution fusion | flops 134217728 | bytes 4587520 | tf_op jit(solution)/shard_map/dot_general | solution.py:13
  21.4 2.8 %fusion.50 = f32[2048,512]{1,0:T(8,128)} fusion(bf16[64,2048]{1,0:T(8,128)(2,1)S(1)} %mul.282, bf16[1,512,256]{2,1,0:T(8,128)(2,1)S(1)} %copy-done.4), kind=kOutput, calls=%fused_computation.118 | convolution fusion | flops 134217728 | bytes 4587520 | tf_op jit(solution)/shard_map/dot_general | solution.py:13
  24.3 2.7 %fusion.46 = f32[2048,512]{1,0:T(8,128)} fusion(bf16[64,2048]{1,0:T(8,128)(2,1)S(1)} %mul.300, bf16[1,512,256]{2,1,0:T(8,128)(2,1)S(1)} %copy-done.4), kind=kOutput, calls=%fused_computation.114 | convolution fusion | flops 134217728 | bytes 4587520 | tf_op jit(solution)/shard_map/dot_general | solution.py:13
  27.0 38.5 %all_gather.3 = bf16[1,4,2,64,512]{4,1,2,0,3:T(4,128)(2,1)S(1)} all-gather(bf16[1,4,2,4,512]{4,1,2,0,3:T(4,128)(2,1)S(1)} %copy.37), channel_id=1, replica_groups=mesh['sub'=8,'sens'=2,'cell'=16] {'cell'}, dimensions={3}, use_global_device_ids=true | all-gather | bytes 557056 | tf_op jit(solution)/shard_map/all_gather | solution.py:93
  65.5 1.4 fusion.69
  66.9 2.0 fusion.65
  69.0 3.1 %fusion.66 = (f32[512,1,8,128]{0,3,2,1:T(8,128)S(1)}, f32[512,1,8,128]{0,3,2,1:T(8,128)S(1)}) fusion(f32[512,2,8,128]{0,3,2,1:T(8,128)} %bitcast.369), kind=kLoop, calls=%fused_computation.151 | loop fusion | bytes 8388608 | tf_op jit(solution)/shard_map/slice | solution.py:24
  72.1 0.4 copy-done.1
  72.5 0.6 fusion.67
  73.1 1.6 copy-done.2
  74.7 0.6 fusion.68
  75.3 2.6 %fusion.40 = (f32[512,128]{0,1:T(8,128)S(1)}, f32[512,128]{0,1:T(8,128)S(1)}, f32[512,128]{0,1:T(8,128)S(1)}, f32[512,128]{0,1:T(8,128)S(1)}) fusion(f32[]{:T(128)} %bitcast.68, f32[128]{0:T(128)S(1)} %convert_multiply_fusion, f32[512]{0:T(512)S(1)} %bitcast.385, f32[512]{0:T(512)S(1)} %bitcast.386, f32[]{:T(128)} %bitcast.50, f32[]{:T(128)} %bitcast.32, ...), kind=kLoop, calls=%fused_computation.105 | loop fusion | flops 393216 | bytes 1053200 | tf_op jit(solution)/shard_map/mul | solution.py:18
  77.9 32.9 %fusion.29 = (bf16[512,1024]{0,1:T(8,128)(2,1)S(1)}, bf16[512,1024]{0,1:T(8,128)(2,1)S(1)}, bf16[512,1024]{0,1:T(8,128)(2,1)S(1)}, bf16[512,1024]{0,1:T(8,128)(2...) fusion(f32[512,1,8,128]{0,3,2,1:T(8,128)S(1)} %copy-done.3, ...), kind=kLoop, calls=%fused_computation.67 | loop fusion | flops 18874368 | bytes 26218496 | tf_op jit(solution)/shard_map/convert_element_type | solution.py:24
  111.2 0.8 convolution_bitcast_fusion
  112.3 0.8 convolution_bitcast_fusion.1
  113.5 0.8 convolution_bitcast_fusion.2
  114.6 0.8 convolution_bitcast_fusion.3
  115.6 4.7 %copy.46 = f32[4,2,64,8,128]{2,3,1,0,4:T(8,128)} copy(f32[4,2,64,8,128]{4,2,3,1,0:T(8,128)S(1)} %pad_maximum_fusion.4) | data formatting | bytes 4194304 | tf_op jit(solution)/shard_map/stack | solution.py:98
  120.4 0.6 copy-done.7
  121.1 0.6 dynamic-slice
  122.3 34.7 %add_reduce_fusion.3 = (f32[8,128]{1,0:T(8,128)S(1)}, f32[8,128]{1,0:T(8,128)S(1)}, f32[8,128]{1,0:T(8,128)S(1)}, f32[8,128]{1,0:T(8,128)S(1)}) fusion(f32[8]{0:T(128)S(1)} %multiply_add_fusion, f32[512,128]{0,1:T(8,128)S(1)} %get-tuple-element.48, f32[512,2,8,128]{0,3,2,1:T(8,128)} %bitcast.365, f32[512,2,8,128]{0,3,2,1:T(8,128)} %bitcast.367, ...), kind=kLoop, calls=%fused_computation.76 | loop fusion | flops 31453184 | bytes 17842208 | tf_op jit(solution)/shard_map/reduce_sum | solution.py:26
  157.0 65.2 %all-reduce = f32[4,8,128]{2,1,0:T(8,128)S(1)} all-reduce(f32[4,8,128]{2,1,0:T(8,128)S(1)} %pad_maximum_fusion.5), channel_id=3, replica_groups=mesh['sub'=8,'sens'=2,'cell'=16] {'sub','sens'}, use_global_device_ids=true, to_apply=%region_6.0.clone | all-reduce | flops 4096 | bytes 32768
  222.2 1.1 fusion.45
  223.3 0.7 fusion.60
  (39 shorter events, 2.1 us)
Async XLA Ops:
  6.5 9.3 %copy-start.4 = (bf16[1,512,256]{2,1,0:T(8,128)(2,1)S(1)}, bf16[1,512,256]{2,1,0:T(8,128)(2,1)}, u32[]{:S(2)}) copy-start(bf16[1,512,256]{2,1,0:T(8,128)(2,1)} %param.9) | copy-start | bytes 786436
  6.5 215.6 %reduce-scatter.3.cloned.1.call-start = ((), (), s32[]{:S(2)}) async-start(), calls=%async_computation.1 | async-start | bytes 4456448 | tf_op jit(solution)/shard_map/reduce_scatter | solution.py:100
  24.3 2.8 %copy-start.6 = (bf16[1,4,2,4,512]{4,3,2,1,0:T(4,128)(2,1)S(1)}, bf16[1,4,2,4,512]{4,3,2,1,0:T(4,128)(2,1)}, u32[]{:S(2)}) copy-start(bf16[1,4,2,4,512]{4,3,2,1,0:T(4,128)(2,1)} %param.8) | copy-start | bytes 98308
  24.3 42.7 %copy-start = (f32[2048,512]{1,0:T(8,128)S(1)}, f32[2048,512]{1,0:T(8,128)}, u32[]{:S(2)}) copy-start(f32[2048,512]{1,0:T(8,128)} %fusion.52) | copy-start | bytes 12582916
  69.0 3.4 %copy-start.1 = (f32[2048,512]{1,0:T(8,128)S(1)}, f32[2048,512]{1,0:T(8,128)}, u32[]{:S(2)}) copy-start(f32[2048,512]{1,0:T(8,128)} %fusion.48) | copy-start | bytes 12582916
  72.5 2.2 copy-start.2
  74.7 3.2 %copy-start.3 = (f32[512,1,8,128]{0,3,2,1:T(8,128)S(1)}, f32[512,1,8,128]{0,3,2,1:T(8,128)}, u32[]{:S(2)}) copy-start(f32[512,1,8,128]{0,3,2,1:T(8,128)} %get-tuple-element.26) | copy-start | bytes 6291460
  112.3 0.9 copy-start.5
  120.4 0.7 copy-start.7
Sparse Core Ops, SparseCore 0:
  120.5 84.2 reduce-scatter.2
where the time goes:
time: 232 us; the launch traced here: 231 us
  blocking collectives  104 us (45%)
  other arithmetic  78.7 us (34%)
  local copies, waits for them, and re-layouts  19.3 us (8%)
  between operations  15 us (6%)
  matrix products  14.2 us (6%)
    unnamed x1, blocking collectives  65.2 us
    all_gather x1, blocking collectives, local(): whole_signal = lax.all_gather(signal, 'cell', axis=3, tiled=True)  38.5 us
    reduce_sum x1, other arithmetic, replica_block(): jnp.sum(jnp.square(real_part.astype(jnp.float32)) + jnp.square(imag_part....  34.7 us
    convert_element_type x1, other arithmetic, replica_block(): (summed[:, 0] * cosine - summed[:, 1] * sine_part).astype(jnp.bfloat16)  32.9 us
    dot_general x4, matrix products, replica_block(): jnp.dot(sensor_rows, modal_block.reshape(mode_total, -1), preferred_eleme...  10.9 us
    slice x4, local copies, waits for them, and re-layouts, replica_block(): summed[:, 0] * cosine - summed[:, 1] * sine_part  6.27 us
    another operation x1, local copies, waits for them, and re-layouts, local(): beams = jnp.stack(per_bin)  4.73 us
  transfers between devices with their start and end apart: 1, of which 0 were waited for; matrix products, arithmetic and copies ran while one was open for 15% of the time, Pallas kernels for 0%

commit v1 on v0

v1 whole, which is shorter than its diff:
```python
import functools

import jax
import jax.numpy as jnp
from jax import lax
from jax.experimental import pallas as pl
from jax.experimental.pallas import tpu as pltpu
from jax.sharding import PartitionSpec as P

range_step = 20.0
depth_step = 2.0
tiny = 1e-06
Z0 = 8
f32 = jnp.float32
bf16 = jnp.bfloat16

NT = (((1,), (1,)), ((), ()))


def replica_kernel(
    bin_index,
    slots,
    counts,
    wave,
    first_range,
    cm,
    sensors,
    curv,
    offs,
    *rest,
):
    out, energy, a32, sums, e0c, e0s, e1c, e1s, esum = rest[-9:]
    modes = cm.shape[3]
    rows = cm.shape[2]
    depth = cm.shape[4]
    blocks = depth // Z0
    phones = sensors.shape[1]
    tile_rows = rows * Z0
    half = blocks * tile_rows

    for part in range(2):
        for row in range(rows):
            turned = cm[0, part, row].astype(f32).T
            a32[part, :, row] = turned.reshape(blocks, Z0, modes)
    lane = lax.broadcasted_iota(jnp.int32, (phones, modes), 1)
    taps = sensors[0, :, bin_index * modes : (bin_index + 1) * modes]
    taps = jnp.where(lane < counts[0, bin_index], taps.astype(f32), 0.0).astype(bf16)
    cells = a32[...].reshape(2 * half, modes).astype(bf16)
    sums[...] = lax.dot_general(cells, taps, NT, preferred_element_type=f32)

    shape = (rows, phones)
    ranges = first_range[0] + range_step * lax.broadcasted_iota(
        jnp.int32, shape, 0
    ).astype(f32)
    k = wave[0, bin_index]
    a = k * curv[...].astype(f32) / ranges
    b = k * (depth_step * offs[...].astype(f32)) / ranges
    zero = lax.broadcasted_iota(jnp.int32, (rows, Z0, phones), 1).astype(f32)
    low = (b[:, None, :] * zero).reshape(tile_rows, phones)
    e0c[...] = jnp.cos(low)
    e0s[...] = -jnp.sin(low)
    pc, ps = jnp.cos(a), jnp.sin(a)
    qc, qs = jnp.cos(Z0 * b), -jnp.sin(Z0 * b)
    for block in range(blocks):
        e1c[block] = pc
        e1s[block] = ps
        pc, ps = pc * qc - ps * qs, pc * qs + ps * qc

    def one_block(block, carry):
        first = pl.multiple_of(block * tile_rows, tile_rows)
        to = pl.multiple_of(slots[block] * tile_rows, tile_rows)
        total = jnp.zeros((tile_rows, 128), f32)
        for tile in range(phones // 128):
            cols = slice(tile * 128, (tile + 1) * 128)
            wide = (rows, Z0, 128)
            hc = jnp.broadcast_to(e1c[block, :, cols][:, None, :], wide).reshape(tile_rows, 128)
            hs = jnp.broadcast_to(e1s[block, :, cols][:, None, :], wide).reshape(tile_rows, 128)
            lc, ls = e0c[:, cols], e0s[:, cols]
            c = hc * lc - hs * ls
            s = hs * lc + hc * ls
            m0 = sums[pl.ds(first, tile_rows), cols]
            m1 = sums[pl.ds(half + first, tile_rows), cols]
            re = (m0 * c - m1 * s).astype(bf16)
            im = (m0 * s + m1 * c).astype(bf16)
            out[0, pl.ds(to, tile_rows), tile * 128 : (tile + 1) * 128] = re
            out[0, pl.ds(to, tile_rows), phones + tile * 128 : phones + (tile + 1) * 128] = im
            re, im = re.astype(f32), im.astype(f32)
            total = total + re * re + im * im
        esum[pl.ds(to, tile_rows), :] = total
        return carry

    lax.fori_loop(0, blocks, one_block, 0)
    total = esum[...]
    high = total.astype(bf16)
    rest_of = (total - high.astype(f32)).astype(bf16)
    ones = jnp.ones((8, 128), bf16)
    energy[...] = lax.dot_general(
        ones, high, NT, preferred_element_type=f32
    ) + lax.dot_general(ones, rest_of, NT, preferred_element_type=f32)


def replicas(bin_index, slots, counts, wave, first_range, cm, sensors, curv, offs, before):
    bins, _, rows, modes, depth = cm.shape
    phones = sensors.shape[1]
    blocks = depth // Z0
    cells = rows * depth
    smem = pl.BlockSpec(memory_space=pltpu.SMEM)
    vmem = pl.BlockSpec(memory_space=pltpu.VMEM)
    in_specs = [
        smem,
        smem,
        smem,
        smem,
        pl.BlockSpec((1, 2, rows, modes, depth), lambda i: (bin_index, 0, 0, 0, 0)),
        vmem,
        vmem,
        vmem,
    ]
    args = [slots, counts, wave, first_range, cm, sensors, curv, offs]
    aliases = {}
    if before is not None:
        in_specs.append(pl.BlockSpec(memory_space=pl.ANY))
        args.append(before)
        aliases = {len(args) - 1: 0}
    return pl.pallas_call(
        functools.partial(replica_kernel, bin_index),
        grid=(1,),
        in_specs=in_specs,
        out_specs=[
            pl.BlockSpec((1, cells, 2 * phones), lambda i: (bin_index, 0, 0)),
            vmem,
        ],
        out_shape=[
            jax.ShapeDtypeStruct((bins, cells, 2 * phones), bf16),
            jax.ShapeDtypeStruct((8, cells), f32),
        ],
        scratch_shapes=[
            pltpu.VMEM((2, blocks, rows, Z0, modes), f32),
            pltpu.VMEM((2 * cells, phones), f32),
            pltpu.VMEM((rows * Z0, phones), f32),
            pltpu.VMEM((rows * Z0, phones), f32),
            pltpu.VMEM((blocks, rows, phones), f32),
            pltpu.VMEM((blocks, rows, phones), f32),
            pltpu.VMEM((cells, 128), f32),
        ],
        input_output_aliases=aliases,
        compiler_params=pltpu.CompilerParams(vmem_limit_bytes=24 * 2**20),
        cost_estimate=pl.CostEstimate(
            flops=4 * cells * phones * modes, bytes_accessed=8 * 2**20, transcendentals=0
        ),
        name="replicas",
    )(*args)


def beam_kernel(pieces, *refs):
    w = refs[0]
    xs = refs[1 : 1 + pieces]
    keep, send = refs[1 + pieces :]
    real = jnp.concatenate([x[0, 0] for x in xs], axis=0)
    imag = jnp.concatenate([x[0, 1] for x in xs], axis=0)
    upper = jnp.concatenate([real, imag], axis=1)
    lower = jnp.concatenate([imag, -real], axis=1)
    signal = jnp.concatenate([upper, lower], axis=0)
    half = w.shape[1] // 2
    kept = lax.dot_general(w[0, :half], signal, NT, preferred_element_type=f32)
    sent = lax.dot_general(w[0, half:], signal, NT, preferred_element_type=f32)
    keep[:, 0] = kept.reshape(keep.shape[0], keep.shape[2], keep.shape[3])
    send[:, 0] = sent.reshape(send.shape[0], send.shape[2], send.shape[3]).astype(bf16)


def beams(w, pieces):
    bins, cells, depth = w.shape
    piece = pieces[0].shape
    looks = 2 * piece[2] * len(pieces)
    owners = 8
    tile_rows = cells // (2 * owners)
    out = (owners, bins, tile_rows, looks)
    block = (owners, 1, tile_rows, looks)
    return pl.pallas_call(
        functools.partial(beam_kernel, len(pieces)),
        grid=(bins,),
        in_specs=[pl.BlockSpec((1, cells, depth), lambda i: (i, 0, 0))]
        + [pl.BlockSpec((1,) + piece[1:], lambda i: (i, 0, 0, 0))] * len(pieces),
        out_specs=[pl.BlockSpec(block, lambda i: (0, i, 0, 0))] * 2,
        out_shape=[jax.ShapeDtypeStruct(out, f32), jax.ShapeDtypeStruct(out, bf16)],
        compiler_params=pltpu.CompilerParams(vmem_limit_bytes=24 * 2**20),
        cost_estimate=pl.CostEstimate(
            flops=2 * bins * cells * depth * looks,
            bytes_accessed=2 * bins * cells * depth,
            transcendentals=0,
        ),
        name="beams",
    )(w, *pieces)


def split(value):
    high = lax.reduce_precision(value, 8, 7)
    return high.astype(bf16), (value - high).astype(bf16)


def local(
    snapshots,
    sensor_modes,
    aperture_curvature,
    depth_offset,
    cell_modes,
    ref_wavenumber,
    range_start,
    mode_counts,
):
    _, bins, modes, _, rows, depth = cell_modes.shape
    blocks = depth // Z0
    cell = lax.axis_index("cell")
    sens = lax.axis_index("sens")
    first_range = range_start + range_step * (cell * rows).astype(f32)
    block_index = jnp.arange(blocks, dtype=jnp.int32)
    slots = ((block_index + sens) % 2) * (blocks // 2) + block_index // 2
    cm = jnp.transpose(cell_modes[0], (0, 2, 3, 1, 4))

    over_x = [(i, (i + 8) % 16) for i in range(16)]
    even = [(i, i ^ 1) for i in range(16)]
    odd = [(i, (i // 8) * 8 + ((i % 8 + (1 if i % 2 else -1)) % 8)) for i in range(16)]

    def after(value, done):
        return lax.optimization_barrier((value, done))[0]

    own = snapshots[0]
    w, energies = None, []

    def one_bin(bin_index, slots, w):
        w, energy = replicas(
            bin_index,
            slots,
            mode_counts,
            ref_wavenumber,
            first_range,
            cm,
            sensor_modes,
            aperture_curvature,
            depth_offset,
            w,
        )
        energies.append(energy[0])
        return w

    cell_pairs = (over_x, even, odd, even, odd)
    held = lax.optimization_barrier(own * jnp.ones((), bf16))
    piece, pieces = own, []
    for turn, pairs in enumerate(cell_pairs):
        got = lax.ppermute(piece, "cell", pairs)
        if turn == 0:
            cm = lax.optimization_barrier(cm)
        else:
            w = one_bin(turn - 1, after(slots, piece), w)
        got, w, cm = lax.optimization_barrier((got, w, cm))
        if turn < 2:
            held = jnp.concatenate([held, got], axis=2)
            piece = held
        else:
            piece = got
        if turn > 0:
            pieces.append(piece)
    energy = jnp.stack(energies).reshape(bins, 2, blocks // 2, rows * Z0)
    energy = jnp.transpose(energy, (1, 2, 0, 3)).reshape(2, blocks // 2, -1, 128)
    energy = energy[0] + lax.ppermute(energy[1], "sens", [(0, 1), (1, 0)])

    keep, send = beams(w, pieces)
    got = lax.ppermute(send, "sens", [(0, 1), (1, 0)])
    total = (keep + got.astype(f32)).astype(bf16)
    owners, looks = total.shape[0], total.shape[3]
    total = total.reshape(owners, -1, looks)
    high, low = split(energy)
    lines = energy.shape[1]
    pad = jnp.zeros((owners, 16 - 2 * lines, looks), bf16)
    total = jnp.concatenate([total, high, low, pad], axis=1)
    parts = lax.all_to_all(total, "sub", 0, 0)
    whole = jnp.sum(parts.astype(f32), axis=0)
    cells = bins * rows * Z0
    beam = whole[:cells]
    energy = (whole[cells : cells + lines] + whole[cells + lines : cells + 2 * lines]).reshape(
        bins, rows, Z0
    )
    power = jnp.sum(jnp.square(beam), axis=1).reshape(bins, rows, Z0) / (looks // 2)
    return 10.0 * jnp.log10((power + tiny) / (energy + tiny))


def solution(mesh):
    return jax.shard_map(
        local,
        mesh=mesh,
        in_specs=(
            P("sub", None, None, "cell", "sens"),
            P("sub", "sens", None),
            P("sub", "sens"),
            P("sub", "sens"),
            P("sub", None, None, None, "cell", None),
            P("sub", None),
            P("sub"),
            P("sub", None),
        ),
        out_specs=P(None, "cell", ("sub", "sens")),
        check_vma=False,
    )
```

time: 232 us -> 56.4 us (0.24)
  blocking collectives: 104 us -> 18.3 us
  other arithmetic: 78.7 us -> 1.34 us
  Pallas kernels: 0 us -> 18.2 us
  local copies, waits for them, and re-layouts: 19.3 us -> 2.09 us
  matrix products: 14.2 us -> 0 us
  between operations: 15 us -> 0.81 us
  starting transfers between devices: 0.01 us -> 11.9 us
  waiting for transfers between devices: 0.02 us -> 2.82 us
    unnamed x1 -> x0, blocking collectives: 65.2 us -> none
    all_gather x1 -> x0, blocking collectives: 38.5 us -> none  [local(): whole_signal = lax.all_gather(signal, 'cell', axis=3, tiled=True)]
    convert_element_type x5 -> x2, other arithmetic: 36.8 us -> 0.17 us  [the longest x1 0.16 us: local(): total = (keep + got.astype(f32)).astype(bf16)]
    reduce_sum x2, other arithmetic: 35.8 us -> 0.19 us  [the longest x1 0.11 us: local(): jnp.sum(jnp.square(beam), axis=1).reshape(bins, rows, Z0) / (looks // 2)]
    all_to_all x0 -> x1, blocking collectives: none -> 18.3 us  [local(): parts = lax.all_to_all(total, 'sub', 0, 0)]
    pallas_call x0 -> x5, Pallas kernels: none -> 18.2 us  [the longest x4 15.3 us: replicas(): pl.pallas_call(functools.partial(replica_kernel, bin_index), grid=(1,), i...]
    dot_general x8 -> x0, matrix products: 14.2 us -> none  [the longest x4 10.9 us: replica_block(): jnp.dot(sensor_rows, modal_block.reshape(mode_total, -1), preferred_eleme...]
    ppermute x0 -> x7, starting transfers between devices: none -> 11.9 us  [the longest x5 11.3 us: local(): got = lax.ppermute(piece, 'cell', pairs)]
  transfers between devices with their start and end apart: 1 -> 7, of which waited for: 0 -> 3; matrix products, arithmetic and copies ran while one was open for 15% -> 4% of each run, Pallas kernels for 0% -> 28%
where the time goes in v1:
time: 56.4 us; the launch traced here: 55.5 us
  blocking collectives  18.3 us (32%)
  Pallas kernels  18.2 us (32%)
  starting transfers between devices  11.9 us (21%)
  waiting for transfers between devices  2.82 us (5%)
  local copies, waits for them, and re-layouts  2.09 us (4%)
  other arithmetic  1.34 us (2%)
  between operations  0.81 us (1%)
    all_to_all x1, blocking collectives, local(): parts = lax.all_to_all(total, 'sub', 0, 0)  18.3 us
    pallas_call x4, Pallas kernels, replicas(): pl.pallas_call(functools.partial(replica_kernel, bin_index), grid=(1,), i...  15.3 us
    ppermute x5, starting transfers between devices, local(): got = lax.ppermute(piece, 'cell', pairs)  11.3 us
    pallas_call x1, Pallas kernels, beams(): pl.pallas_call(functools.partial(beam_kernel, len(pieces)), grid=(bins,),...  2.92 us
    ppermute x5, waiting for transfers between devices, local(): got = lax.ppermute(piece, 'cell', pairs)  1.81 us
    unnamed x13, local copies, waits for them, and re-layouts  1.56 us
  transfers between devices with their start and end apart: 7, of which 3 were waited for; matrix products, arithmetic and copies ran while one was open for 4% of the time, Pallas kernels for 28%

profile of v1, /device:TPU:2, one launch (start us, length us, event | category | flops | bytes accessed | tf_op | source)
XLA Modules:
  0.0 55.5 jit_solution(11062804634917857720)
XLA Ops:
  0.0 2.3 %collective-permute-start = (bf16[4,2,4,512]{3,2,1,0:T(4,128)(2,1)}, bf16[4,2,4,512]{3,2,1,0:T(4,128)(2,1)S(1)}, u32[]{:S(2)}, u32[]{:S(2)}) collective-permute-start(bf16[4,2,4,512]{3,2,1,0:T(4,128)(2,1)} %bitcast.15), channel_id=1, source_target_pairs={{0,8},{1,9},{2,10},{3,11},{4,12},{5,13},{6,14},{7,15},{8,0},{9,1},... | collective-permute-start | bytes 98312 | tf_op jit(solution)/shard_map/ppermute | solution.py:250
  2.3 1.5 %copy.16 = bf16[1,4,64,2,8,128]{5,2,4,3,1,0:T(8,128)(2,1)S(1)} copy(bf16[1,4,64,2,8,128]{5,4,3,2,1,0:T(8,128)(2,1)} %param.12) | data formatting | bytes 2097152 | tf_op args[4]
  3.8 0.6 %collective-permute-done = bf16[4,2,4,512]{3,2,1,0:T(4,128)(2,1)S(1)} collective-permute-done((bf16[4,2,4,512]{3,2,1,0:T(4,128)(2,1)}, bf16[4,2,4,512]{3,2,1,0:T(4,128)(2,1)S(1)}, u32[]{:S(2)}, u32[]{:S(2)}) %collective-permute-start) | collective-permute-done | bytes 32800 | tf_op jit(solution)/shard_map/ppermute | solution.py:250
  4.5 1.7 %collective-permute-start.1 = (bf16[4,2,8,512]{3,2,1,0:T(8,128)(2,1)S(1)}, bf16[4,2,8,512]{3,2,1,0:T(8,128)(2,1)S(1)}, u32[]{:S(2)}, u32[]{:S(2)}) collective-permute-start(bf16[4,2,8,512]{3,2,1,0:T(8,128)(2,1)S(1)} %pad_maximum_fusion.1), channel_id=1, source_target_pairs={{0,1},{1,0},{2,3},{3,2},{4,5},{5,4},{6,7},{7,6},{8,9},{9,8},{10,11... | collective-permute-start | bytes 196616 | tf_op jit(solution)/shard_map/ppermute | solution.py:250
  6.9 3.8 %replicas.4 = (bf16[4,1024,1024]{2,1,0:T(8,128)(2,1)S(1)}, f32[8,1024]{1,0:T(8,128)S(1)}) custom-call(s32[16]{0:T(128)S(1)} %fusion.3.slots, s32[1,4]{1,0:T(1,128)S(1)} %copy-done.3, f32[1,4]{1,0:T(1,128)S(1)} %copy-done.4, f32[1]{0:T(128)S(6)} %add.48.first_range, bf16[4,2,8,64,128]{4,3,2,1,0:T(8,128)(2,1)S(1)} %bitcast.9, ...), custom_call_target="tpu_custom_call" | custom-call | flops 134217728 | bytes 8388608 | tf_op jit(solution)/shard_map/replicas/pallas_call | solution.py:125
  10.7 0.0 collective-permute-done.1
  10.7 0.1 pad_maximum_fusion.refs_1_
  10.8 5.0 %collective-permute-start.2 = (bf16[4,2,16,512]{3,2,1,0:T(8,128)(2,1)S(1)}, bf16[4,2,16,512]{3,2,1,0:T(8,128)(2,1)S(1)}, u32[]{:S(2)}, u32[]{:S(2)}) collective-permute-start(bf16[4,2,16,512]{3,2,1,0:T(8,128)(2,1)S(1)} %pad_maximum_fusion.refs_1_), channel_id=1, source_target_pairs={{0,7},{1,2},{2,1},{3,4},{4,3},{5,6},{6,5},{7,0},{8,15},{9,10},{10,... | collective-permute-start | bytes 393224 | tf_op jit(solution)/shard_map/ppermute | solution.py:250
  15.8 3.8 %replicas.5 = (bf16[4,1024,1024]{2,1,0:T(8,128)(2,1)S(1)}, f32[8,1024]{1,0:T(8,128)S(1)}) custom-call(s32[16]{0:T(128)S(1)} %fusion.3.slots, s32[1,4]{1,0:T(1,128)S(1)} %copy-done.3, f32[1,4]{1,0:T(1,128)S(1)} %copy-done.4, f32[1]{0:T(128)S(6)} %add.48.first_range, bf16[4,2,8,64,128]{4,3,2,1,0:T(8,128)(2,1)S(1)} %bitcast.10, ...), custom_call_target="tpu_custom_call", output_to_operand_aliasing={{0}: (8, {})} | custom-call | flops 134217728 | bytes 8388608 | tf_op jit(solution)/shard_map/replicas/pallas_call | solution.py:125
  19.7 0.0 collective-permute-done.2.refs_2_
  19.7 0.1 collective-permute-start.3
  19.7 3.8 %replicas.6 = (bf16[4,1024,1024]{2,1,0:T(8,128)(2,1)S(1)}, f32[8,1024]{1,0:T(8,128)S(1)}) custom-call(s32[16]{0:T(128)S(1)} %fusion.3.slots, s32[1,4]{1,0:T(1,128)S(1)} %copy-done.3, f32[1,4]{1,0:T(1,128)S(1)} %copy-done.4, f32[1]{0:T(128)S(6)} %add.48.first_range, bf16[4,2,8,64,128]{4,3,2,1,0:T(8,128)(2,1)S(1)} %bitcast.11, ...), custom_call_target="tpu_custom_call", output_to_operand_aliasing={{0}: (8, {})} | custom-call | flops 134217728 | bytes 8388608 | tf_op jit(solution)/shard_map/replicas/pallas_call | solution.py:125
  23.5 1.1 %collective-permute-done.3.refs_3_ = bf16[4,2,16,512]{3,2,1,0:T(8,128)(2,1)S(1)} collective-permute-done((bf16[4,2,16,512]{3,2,1,0:T(8,128)(2,1)S(1)}, bf16[4,2,16,512]{3,2,1,0:T(8,128)(2,1)S(1)}, u32[]{:S(2)}, u32[]{:S(2)}) %collective-permute-start.3) | collective-permute-done | bytes 131104 | tf_op jit(solution)/shard_map/ppermute | solution.py:250
  24.7 2.3 %collective-permute-start.4 = (bf16[4,2,16,512]{3,2,1,0:T(8,128)(2,1)S(1)}, bf16[4,2,16,512]{3,2,1,0:T(8,128)(2,1)S(1)}, u32[]{:S(2)}, u32[]{:S(2)}) collective-permute-start(bf16[4,2,16,512]{3,2,1,0:T(8,128)(2,1)S(1)} %collective-permute-done.3.refs_3_), channel_id=1, source_target_pairs={{0,7},{1,2},{2,1},{3,4},{4,3},{5,6},{6,5},{7,0},{8,15},{9,10},{10,... | collective-permute-start | bytes 393224 | tf_op jit(solution)/shard_map/ppermute | solution.py:250
  27.0 3.8 %replicas.7 = (bf16[4,1024,1024]{2,1,0:T(8,128)(2,1)S(1)}, f32[8,1024]{1,0:T(8,128)S(1)}) custom-call(s32[16]{0:T(128)S(1)} %fusion.3.slots, s32[1,4]{1,0:T(1,128)S(1)} %copy-done.3, f32[1,4]{1,0:T(1,128)S(1)} %copy-done.4, f32[1]{0:T(128)S(6)} %add.48.first_range, bf16[4,2,8,64,128]{4,3,2,1,0:T(8,128)(2,1)S(1)} %bitcast.12, ...), custom_call_target="tpu_custom_call", output_to_operand_aliasing={{0}: (8, {})} | custom-call | flops 134217728 | bytes 8388608 | tf_op jit(solution)/shard_map/replicas/pallas_call | solution.py:125
  30.8 0.0 collective-permute-done.4.refs_4_
  30.9 2.9 %beams.1 = (f32[8,4,64,128]{3,2,1,0:T(8,128)S(1)}, bf16[8,4,64,128]{3,2,1,0:T(8,128)(2,1)S(1)}) custom-call(bf16[4,1024,1024]{2,1,0:T(8,128)(2,1)S(1)} %get-tuple-element.51.refs_0_, bf16[4,2,16,512]{3,2,1,0:T(8,128)(2,1)S(1)} %pad_maximum_fusion.refs_1_, bf16[4,2,16,512]{3,2,1,0:T(8,128)(2,1)S(1)} %collective-permute-done.2.refs_2_, ...), custom_call_target="tpu_custom_call" | custom-call | flops 1073741824 | bytes 8388608 | tf_op jit(solution)/shard_map/beams/pallas_call | solution.py:179
  33.8 0.1 collective-permute-start.5
  33.9 0.1 reshape.20
  34.0 0.1 squeeze.15
  34.1 0.5 collective-permute-start.6
  34.6 0.1 pad.3.clone
  34.7 0.1 squeeze.14
  34.8 1.0 %collective-permute-done.6 = f32[8,2,128]{2,1,0:T(2,128)S(1)} collective-permute-done((f32[8,2,128]{2,1,0:T(2,128)S(1)}, f32[8,2,128]{2,1,0:T(2,128)S(1)}, u32[]{:S(2)}, u32[]{:S(2)}) %collective-permute-start.6) | collective-permute-done | bytes 8224 | tf_op jit(solution)/shard_map/ppermute | solution.py:265
  35.8 0.2 add_convert_fusion
  36.0 0.2 maximum_maximum_fusion
  36.2 18.3 %all_to_all.5 = bf16[8,272,128]{2,1,0:T(8,128)(2,1)S(1)} all-to-all(bf16[8,272,128]{2,1,0:T(8,128)(2,1)S(1)} %maximum_maximum_fusion), channel_id=1, replica_groups=mesh['sub'=8,'sens'=2,'cell'=16] {'sub'}, dimensions={0} | all-to-all | bytes 1114112 | tf_op jit(solution)/shard_map/all_to_all | solution.py:276
  54.5 0.1 convert_reduce_fusion
  54.6 0.1 fusion
  54.7 0.1 add.52
  54.8 0.1 add.55
  54.8 0.6 %log_multiply_fusion = f32[4,8,8]{2,1,0:T(8,128)} fusion(f32[4,8,8]{2,1,0:T(8,128)S(1)} %add.52, f32[4,8,8]{2,1,0:T(8,128)S(1)} %add.55), kind=kLoop, calls=%fused_computation.9 | loop fusion | flops 512 | bytes 3072 | tf_op jit(solution)/shard_map/mul | solution.py:284
  (27 shorter events, 0.2 us)
Async XLA Ops:
  0.0 4.4 %copy-start.5 = (bf16[1,4,2,4,512]{4,3,2,1,0:T(4,128)(2,1)S(1)}, bf16[1,4,2,4,512]{4,3,2,1,0:T(4,128)(2,1)}, u32[]{:S(2)}) copy-start(bf16[1,4,2,4,512]{4,3,2,1,0:T(4,128)(2,1)} %param.8) | copy-start | bytes 98308
  0.0 4.4 %collective-permute-start = (bf16[4,2,4,512]{3,2,1,0:T(4,128)(2,1)}, bf16[4,2,4,512]{3,2,1,0:T(4,128)(2,1)S(1)}, u32[]{:S(2)}, u32[]{:S(2)}) collective-permute-start(bf16[4,2,4,512]{3,2,1,0:T(4,128)(2,1)} %bitcast.15), channel_id=1, source_target_pairs={{0,8},{1,9},{2,10},{3,11},{4,12},{5,13},{6,14},{7,15},{8,0},{9,1},... | collective-permute-start | bytes 98312 | tf_op jit(solution)/shard_map/ppermute | solution.py:250
  2.3 4.6 %copy-start = (bf16[1,512,256]{2,1,0:T(8,128)(2,1)S(1)}, bf16[1,512,256]{2,1,0:T(8,128)(2,1)}, u32[]{:S(2)}) copy-start(bf16[1,512,256]{2,1,0:T(8,128)(2,1)} %sensors.7) | copy-start | bytes 786436
  2.3 4.6 %copy-start.1 = (bf16[1,512]{1,0:T(2,128)(2,1)S(1)}, bf16[1,512]{1,0:T(2,128)(2,1)}, u32[]{:S(2)}) copy-start(bf16[1,512]{1,0:T(2,128)(2,1)} %curv.7) | copy-start | bytes 3076
  2.3 4.6 %copy-start.2 = (bf16[1,512]{1,0:T(2,128)(2,1)S(1)}, bf16[1,512]{1,0:T(2,128)(2,1)}, u32[]{:S(2)}) copy-start(bf16[1,512]{1,0:T(2,128)(2,1)} %offs.7) | copy-start | bytes 3076
  2.3 4.6 %copy-start.3 = (s32[1,4]{1,0:T(1,128)S(1)}, s32[1,4]{1,0:T(1,128)}, u32[]{:S(2)}) copy-start(s32[1,4]{1,0:T(1,128)} %counts.7) | copy-start | bytes 52
  2.3 4.6 %copy-start.4 = (f32[1,4]{1,0:T(1,128)S(1)}, f32[1,4]{1,0:T(1,128)}, u32[]{:S(2)}) copy-start(f32[1,4]{1,0:T(1,128)} %wave.7) | copy-start | bytes 52
  4.5 6.2 %collective-permute-start.1 = (bf16[4,2,8,512]{3,2,1,0:T(8,128)(2,1)S(1)}, bf16[4,2,8,512]{3,2,1,0:T(8,128)(2,1)S(1)}, u32[]{:S(2)}, u32[]{:S(2)}) collective-permute-start(bf16[4,2,8,512]{3,2,1,0:T(8,128)(2,1)S(1)} %pad_maximum_fusion.1), channel_id=1, source_target_pairs={{0,1},{1,0},{2,3},{3,2},{4,5},{5,4},{6,7},{7,6},{8,9},{9,8},{10,11... | collective-permute-start | bytes 196616 | tf_op jit(solution)/shard_map/ppermute | solution.py:250
  10.8 8.9 %collective-permute-start.2 = (bf16[4,2,16,512]{3,2,1,0:T(8,128)(2,1)S(1)}, bf16[4,2,16,512]{3,2,1,0:T(8,128)(2,1)S(1)}, u32[]{:S(2)}, u32[]{:S(2)}) collective-permute-start(bf16[4,2,16,512]{3,2,1,0:T(8,128)(2,1)S(1)} %pad_maximum_fusion.refs_1_), channel_id=1, source_target_pairs={{0,7},{1,2},{2,1},{3,4},{4,3},{5,6},{6,5},{7,0},{8,15},{9,10},{10,... | collective-permute-start | bytes 393224 | tf_op jit(solution)/shard_map/ppermute | solution.py:250
  19.7 5.0 %collective-permute-start.3 = (bf16[4,2,16,512]{3,2,1,0:T(8,128)(2,1)S(1)}, bf16[4,2,16,512]{3,2,1,0:T(8,128)(2,1)S(1)}, u32[]{:S(2)}, u32[]{:S(2)}) collective-permute-start(bf16[4,2,16,512]{3,2,1,0:T(8,128)(2,1)S(1)} %collective-permute-done.2.refs_2_), channel_id=1, source_target_pairs={{0,1},{1,0},{2,3},{3,2},{4,5},{5,4},{6,7},{7,6},{8,9},{9,8},{10,11... | collective-permute-start | bytes 393224 | tf_op jit(solution)/shard_map/ppermute | solution.py:250
  24.7 6.2 %collective-permute-start.4 = (bf16[4,2,16,512]{3,2,1,0:T(8,128)(2,1)S(1)}, bf16[4,2,16,512]{3,2,1,0:T(8,128)(2,1)S(1)}, u32[]{:S(2)}, u32[]{:S(2)}) collective-permute-start(bf16[4,2,16,512]{3,2,1,0:T(8,128)(2,1)S(1)} %collective-permute-done.3.refs_3_), channel_id=1, source_target_pairs={{0,7},{1,2},{2,1},{3,4},{4,3},{5,6},{6,5},{7,0},{8,15},{9,10},{10,... | collective-permute-start | bytes 393224 | tf_op jit(solution)/shard_map/ppermute | solution.py:250
  33.8 2.0 %collective-permute-start.5 = (bf16[8,4,64,128]{3,2,1,0:T(8,128)(2,1)S(1)}, bf16[8,4,64,128]{3,2,1,0:T(8,128)(2,1)S(1)}, u32[]{:S(2)}, u32[]{:S(2)}) collective-permute-start(bf16[8,4,64,128]{3,2,1,0:T(8,128)(2,1)S(1)} %get-tuple-element.54), channel_id=1, source_target_pairs={{0,16},{16,0},{1,17},{17,1},{2,18},{18,2},{3,19},{19,3},{4,20},{20... | collective-permute-start | bytes 1572872 | tf_op jit(solution)/shard_map/ppermute | solution.py:268
  34.1 1.7 %collective-permute-start.6 = (f32[8,2,128]{2,1,0:T(2,128)S(1)}, f32[8,2,128]{2,1,0:T(2,128)S(1)}, u32[]{:S(2)}, u32[]{:S(2)}) collective-permute-start(f32[8,2,128]{2,1,0:T(2,128)S(1)} %squeeze.15), channel_id=1, source_target_pairs={{0,16},{16,0},{1,17},{17,1},{2,18},{18,2},{3,19},{19,3},{4,20},{20... | collective-permute-start | bytes 24584 | tf_op jit(solution)/shard_map/ppermute | solution.py:265

commit v2 on v1

v2 whole, which is shorter than its diff:
```python
import functools

import jax
import jax.numpy as jnp
from jax import lax
from jax.experimental import pallas as pl
from jax.experimental.pallas import tpu as pltpu
from jax.sharding import PartitionSpec as P

range_step = 20.0
depth_step = 2.0
tiny = 1e-06
Z0 = 8
f32 = jnp.float32
bf16 = jnp.bfloat16

NT = (((1,), (1,)), ((), ()))


def small_sincos(r):
    t = r * r
    s = r + r * t * (-1.6666654611e-1 + t * (8.3321608736e-3 - t * 1.9515295891e-4))
    c = t * t * (4.166664568298827e-2 + t * (-1.388731625493765e-3 + t * 2.443315711809948e-5))
    return s, 1.0 - 0.5 * t + c


def sincos(x):
    turn = jnp.floor(x * 0.6366197723675814 + 0.5)
    r = ((x - turn * 1.5703125) - turn * 4.837512969970703e-4) - turn * 7.54978995489188e-8
    q = turn.astype(jnp.int32)
    s, c = small_sincos(r)
    odd = (q & 1) == 1
    sine, cosine = jnp.where(odd, c, s), jnp.where(odd, s, c)
    sine = jnp.where((q & 2) == 2, -sine, sine)
    cosine = jnp.where(((q + 1) & 2) == 2, -cosine, cosine)
    return sine, cosine


def replica_kernel(
    bin_index,
    slots,
    counts,
    wave,
    first_range,
    cm,
    sensors,
    curv,
    offs,
    *rest,
):
    out, energy, a32, sums, now_c, now_s, old_c, old_s, twice, esum, placed = rest
    modes = cm.shape[3]
    rows = cm.shape[2]
    depth = cm.shape[4]
    blocks = depth // Z0
    phones = sensors.shape[1]
    tile_rows = rows * Z0
    half = blocks * tile_rows

    for part in range(2):
        for row in range(rows):
            turned = cm[bin_index, part, row].astype(f32).T
            a32[part, :, row] = turned.reshape(blocks, Z0, modes)
    lane = lax.broadcasted_iota(jnp.int32, (phones, modes), 1)
    taps = sensors[0, :, bin_index * modes : (bin_index + 1) * modes]
    taps = jnp.where(lane < counts[0, bin_index], taps.astype(f32), 0.0).astype(bf16)
    cells = a32[...].reshape(2 * half, modes).astype(bf16)
    sums[...] = lax.dot_general(cells, taps, NT, preferred_element_type=f32)

    shape = (rows, phones)
    ranges = first_range[0] + range_step * lax.broadcasted_iota(
        jnp.int32, shape, 0
    ).astype(f32)
    k = wave[0, bin_index]
    a = k * curv[...].astype(f32) / ranges
    b = k * (depth_step * offs[...].astype(f32)) / ranges
    zero = lax.broadcasted_iota(jnp.int32, (rows, Z0, phones), 1).astype(f32)
    wide = (rows, Z0, phones)

    def spread(value):
        return jnp.broadcast_to(value[:, None, :], wide).reshape(tile_rows, phones)

    low_s, low_c = small_sincos((b[:, None, :] * zero).reshape(tile_rows, phones))
    high_s, high_c = (spread(v) for v in sincos(a))
    step_s, step_c = small_sincos(Z0 * b)
    c, s = high_c * low_c + high_s * low_s, high_s * low_c - high_c * low_s
    now_c[...], now_s[...] = c, s
    twice[...] = spread(2.0 * step_c)
    step_s, step_c = spread(step_s), spread(step_c)
    old_c[...], old_s[...] = c * step_c - s * step_s, s * step_c + c * step_s

    def one_pair(pair, carry):
        here = pl.ds(pl.multiple_of(pair * 2 * Z0, 2 * Z0), 2 * Z0)
        tiles = phones // 128
        group = 4
        for lead in range(0, tiles, group):
            spans = [slice(i * 128, (i + 1) * 128) for i in range(lead, lead + group)]
            turns = [(now_c[here, at], now_s[here, at]) for at in spans]
            before = [(old_c[here, at], old_s[here, at]) for at in spans]
            steps = [twice[here, at] for at in spans]
            for block in range(blocks):
                first = pl.multiple_of(block * tile_rows + pair * 2 * Z0, 2 * Z0)
                to = pl.multiple_of(slots[block] * tile_rows + pair * 2 * Z0, 2 * Z0)
                power = jnp.zeros((2 * Z0, 128), f32) if lead == 0 else esum[pl.ds(first, 2 * Z0), :]
                for i, at in enumerate(spans):
                    c, s = turns[i]
                    m0 = sums[pl.ds(first, 2 * Z0), at]
                    m1 = sums[pl.ds(half + first, 2 * Z0), at]
                    re = (m0 * c - m1 * s).astype(bf16)
                    im = (m0 * s + m1 * c).astype(bf16)
                    out[pl.ds(to, 2 * Z0), at] = re
                    out[pl.ds(to, 2 * Z0), phones + at.start : phones + at.stop] = im
                    power = power + (m0 * m0 + m1 * m1)
                    turns[i] = (steps[i] * c - before[i][0], steps[i] * s - before[i][1])
                    before[i] = (c, s)
                esum[pl.ds(first, 2 * Z0), :] = power
        return carry

    lax.fori_loop(0, rows // 2, one_pair, 0, unroll=True)
    for block in range(blocks):
        to = pl.multiple_of(slots[block] * tile_rows, tile_rows)
        placed[pl.ds(to, tile_rows), :] = esum[block * tile_rows : (block + 1) * tile_rows, :]
    total = placed[...]
    high = total.astype(bf16)
    rest_of = (total - high.astype(f32)).astype(bf16)
    ones = jnp.ones((8, 128), bf16)
    energy[...] = lax.dot_general(
        ones, high, NT, preferred_element_type=f32
    ) + lax.dot_general(ones, rest_of, NT, preferred_element_type=f32)


def replicas(bin_index, slots, counts, wave, first_range, cm, sensors, curv, offs):
    bins, _, rows, modes, depth = cm.shape
    phones = sensors.shape[1]
    blocks = depth // Z0
    cells = rows * depth
    smem = pl.BlockSpec(memory_space=pltpu.SMEM)
    vmem = pl.BlockSpec(memory_space=pltpu.VMEM)
    return pl.pallas_call(
        functools.partial(replica_kernel, bin_index),
        in_specs=[smem] * 4 + [vmem] * 4,
        out_specs=[vmem] * 2,
        out_shape=[
            jax.ShapeDtypeStruct((cells, 2 * phones), bf16),
            jax.ShapeDtypeStruct((8, cells), f32),
        ],
        scratch_shapes=[
            pltpu.VMEM((2, blocks, rows, Z0, modes), f32),
            pltpu.VMEM((2 * cells, phones), f32),
            *[pltpu.VMEM((rows * Z0, phones), f32)] * 5,
            *[pltpu.VMEM((cells, 128), f32)] * 2,
        ],
        compiler_params=pltpu.CompilerParams(vmem_limit_bytes=24 * 2**20),
        cost_estimate=pl.CostEstimate(
            flops=4 * cells * phones * modes, bytes_accessed=8 * 2**20, transcendentals=0
        ),
        name="replicas",
    )(slots, counts, wave, first_range, cm, sensors, curv, offs)


def beam_kernel(bins, *refs):
    ws, xs = refs[:bins], refs[bins:-2]
    keep, send = refs[-2:]
    for b, w in enumerate(ws):
        real = jnp.concatenate([x[b, 0] for x in xs], axis=0)
        imag = jnp.concatenate([x[b, 1] for x in xs], axis=0)
        upper = jnp.concatenate([real, imag], axis=1)
        lower = jnp.concatenate([imag, -real], axis=1)
        signal = jnp.concatenate([upper, lower], axis=0)
        half = w.shape[0] // 2
        kept = lax.dot_general(w[:half], signal, NT, preferred_element_type=f32)
        sent = lax.dot_general(w[half:], signal, NT, preferred_element_type=f32)
        keep[:, b] = kept.reshape(keep.shape[0], keep.shape[2], keep.shape[3])
        send[:, b] = sent.reshape(send.shape[0], send.shape[2], send.shape[3]).astype(bf16)


def beams(ws, pieces):
    bins = len(ws)
    cells, depth = ws[0].shape
    looks = 2 * pieces[0].shape[2] * len(pieces)
    owners = 8
    out = (owners, bins, cells // (2 * owners), looks)
    vmem = pl.BlockSpec(memory_space=pltpu.VMEM)
    return pl.pallas_call(
        functools.partial(beam_kernel, bins),
        in_specs=[vmem] * (bins + len(pieces)),
        out_specs=[vmem] * 2,
        out_shape=[jax.ShapeDtypeStruct(out, f32), jax.ShapeDtypeStruct(out, bf16)],
        compiler_params=pltpu.CompilerParams(vmem_limit_bytes=24 * 2**20),
        cost_estimate=pl.CostEstimate(
            flops=2 * bins * cells * depth * looks,
            bytes_accessed=2 * bins * cells * depth,
            transcendentals=0,
        ),
        name="beams",
    )(*ws, *pieces)


def split(value):
    high = lax.reduce_precision(value, 8, 7)
    return high.astype(bf16), (value - high).astype(bf16)


def local(
    snapshots,
    sensor_modes,
    aperture_curvature,
    depth_offset,
    cell_modes,
    ref_wavenumber,
    range_start,
    mode_counts,
):
    _, bins, modes, _, rows, depth = cell_modes.shape
    blocks = depth // Z0
    cell = lax.axis_index("cell")
    sens = lax.axis_index("sens")
    first_range = range_start + range_step * (cell * rows).astype(f32)
    block_index = jnp.arange(blocks, dtype=jnp.int32)
    sub = lax.axis_index("sub")

    away = block_index ^ (2 * sub + sens)
    slots = 8 * (away % 2) + 2 * ((away // 2) % 4) + away // 8
    cm = jnp.transpose(cell_modes[0], (0, 2, 3, 1, 4))

    def after(value, done):
        return lax.optimization_barrier((value, done))[0]

    own = snapshots[0]
    ws, energies = [], []

    def one_bin(bin_index, slots):
        w, energy = replicas(
            bin_index,
            slots,
            mode_counts,
            ref_wavenumber,
            first_range,
            cm,
            sensor_modes,
            aperture_curvature,
            depth_offset,
        )
        ws.append(w)
        energies.append(energy[0])

    def from_cell(piece, flip):
        return lax.ppermute(piece, "cell", [(i, i ^ flip) for i in range(16)])

    held = lax.optimization_barrier(own * jnp.ones((), bf16))
    gots = [from_cell(own, flip) for flip in (4, 6, 2)]
    one_bin(0, slots)
    gots, ws[0] = lax.optimization_barrier((gots, ws[0]))
    piece = jnp.concatenate([held, *gots], axis=2)
    gots = [from_cell(piece, flip) for flip in (9, 8, 1)]
    for bin_index in range(1, bins):
        one_bin(bin_index, after(slots, piece))
    gots, ws = lax.optimization_barrier((gots, ws))
    pieces = [piece, *gots]
    energy = jnp.stack(energies).reshape(bins, 2, blocks // 2, rows * Z0)
    energy = jnp.transpose(energy, (1, 2, 0, 3)).reshape(2, blocks // 2, -1, 128)
    energy = energy[0] + lax.ppermute(energy[1], "sens", [(0, 1), (1, 0)])

    keep, send = beams(ws, pieces)
    swap = [(0, 1), (1, 0)]
    got = lax.ppermute(send, "sens", swap)
    beam = keep + got.astype(f32)
    owners, looks = beam.shape[0], beam.shape[3]
    beam = beam.reshape(owners, -1, looks)
    cells, lines = beam.shape[1], energy.shape[1]
    def sent(part):
        high, low = split(energy[part])
        return jnp.concatenate([beam[part].astype(bf16), high, low], axis=1)

    def summed(total, got):
        beam, energy = total
        got = got.astype(f32)
        return (
            beam + got[:, :cells],
            energy + got[:, cells : cells + lines] + got[:, cells + lines :],
        )

    total = beam[0:2], energy[0:2]
    gots = [
        lax.ppermute(sent(slice(2 * k, 2 * k + 2)), "sub", [(i, i ^ k) for i in range(8)])
        for k in (2, 3, 1)
    ]
    for got in gots:
        total = summed(total, got)
    beam, energy = total
    got = lax.ppermute(sent(slice(1, 2)), "sub", [(i, i ^ 4) for i in range(8)])
    beam, energy = summed((beam[0:1], energy[0:1]), got)
    energy = energy.reshape(bins, rows, Z0)
    power = jnp.sum(jnp.square(beam[0]), axis=1).reshape(bins, rows, Z0) / (looks // 2)
    return 10.0 * jnp.log10((power + tiny) / (energy + tiny))


def solution(mesh):
    return jax.shard_map(
        local,
        mesh=mesh,
        in_specs=(
            P("sub", None, None, "cell", "sens"),
            P("sub", "sens", None),
            P("sub", "sens"),
            P("sub", "sens"),
            P("sub", None, None, None, "cell", None),
            P("sub", None),
            P("sub"),
            P("sub", None),
        ),
        out_specs=P(None, "cell", ("sub", "sens")),
        check_vma=False,
    )
```

time: 56.4 us -> 48.8 us (0.87); the launches traced: 55.5 us -> 48.7 us
  blocking collectives: 18.3 us -> 0 us
  waiting for transfers between devices: 2.82 us -> 11.4 us
  starting transfers between devices: 11.9 us -> 19.9 us
  Pallas kernels: 18.2 us -> 13.1 us
    all_to_all x1 -> x0, blocking collectives: 18.3 us -> none  [local(): parts = lax.all_to_all(total, 'sub', 0, 0)]
    ppermute x6 -> x11, waiting for transfers between devices: 1.82 us -> 10.3 us  [the longest x3 6.39 us: local(): lax.ppermute(sent(slice(2 * k, 2 * k + 2)), 'sub', [(i, i ^ k) for i in r...]
    ppermute x6 -> x11, starting transfers between devices: 11.4 us -> 19.4 us  [the longest x6 12.3 us: from_cell(): return lax.ppermute(piece, 'cell', [(i, i ^ flip) for i in range(16)])]
    pallas_call x5, Pallas kernels: 18.2 us -> 13.1 us  [the longest x4 10.8 us: replicas(): pl.pallas_call(functools.partial(replica_kernel, bin_index), in_specs=[sm...]
  transfers between devices with their start and end apart: 7 -> 12, of which waited for: 3 -> 5; matrix products, arithmetic and copies ran while one was open for 4% -> 4% of each run, Pallas kernels for 28% -> 22%
where the time goes in v2:
time: 48.8 us; the launch traced here: 48.7 us
  starting transfers between devices  19.9 us (41%)
  Pallas kernels  13.1 us (27%)
  waiting for transfers between devices  11.4 us (23%)
  local copies, waits for them, and re-layouts  2.03 us (4%)
  other arithmetic  1.34 us (3%)
  between operations  0.91 us (2%)
    ppermute x6, starting transfers between devices, from_cell(): return lax.ppermute(piece, 'cell', [(i, i ^ flip) for i in range(16)])  12.3 us
    pallas_call x4, Pallas kernels, replicas(): pl.pallas_call(functools.partial(replica_kernel, bin_index), in_specs=[sm...  10.8 us
    ppermute x3, waiting for transfers between devices, local(): lax.ppermute(sent(slice(2 * k, 2 * k + 2)), 'sub', [(i, i ^ k) for i in r...  6.39 us
    ppermute x3, starting transfers between devices, local(): lax.ppermute(sent(slice(2 * k, 2 * k + 2)), 'sub', [(i, i ^ k) for i in r...  4.77 us
    ppermute x1, waiting for transfers between devices, local(): got = lax.ppermute(sent(slice(1, 2)), 'sub', [(i, i ^ 4) for i in range(8)])  3.67 us
    pallas_call x1, Pallas kernels, beams(): pl.pallas_call(functools.partial(beam_kernel, bins), in_specs=[vmem] * (b...  2.32 us
    ppermute x1, starting transfers between devices, local(): got = lax.ppermute(sent(slice(1, 2)), 'sub', [(i, i ^ 4) for i in range(8)])  2.21 us
    unnamed x13, local copies, waits for them, and re-layouts  1.52 us
  transfers between devices with their start and end apart: 12, of which 5 were waited for; matrix products, arithmetic and copies ran while one was open for 4% of the time, Pallas kernels for 22%

profile of v2, /device:TPU:2, one launch (start us, length us, event | category | flops | bytes accessed | tf_op | source)
XLA Modules:
  0.0 48.7 jit_solution(10214309446480644011)
XLA Ops:
  0.0 7.3 %collective-permute-start = (bf16[4,2,4,512]{3,2,1,0:T(4,128)(2,1)}, bf16[4,2,4,512]{3,2,1,0:T(4,128)(2,1)S(1)}, u32[]{:S(2)}, u32[]{:S(2)}) collective-permute-start(bf16[4,2,4,512]{3,2,1,0:T(4,128)(2,1)} %bitcast.21), channel_id=1, source_target_pairs={{0,4},{1,5},{2,6},{3,7},{4,0},{5,1},{6,2},{7,3},{8,12},{9,13},{10,... | collective-permute-start | bytes 98312 | tf_op jit(solution)/shard_map/ppermute | solution.py:248
  7.3 1.5 %collective-permute-start.2 = (bf16[4,2,4,512]{3,2,1,0:T(4,128)(2,1)}, bf16[4,2,4,512]{3,2,1,0:T(4,128)(2,1)S(1)}, u32[]{:S(2)}, u32[]{:S(2)}) collective-permute-start(bf16[4,2,4,512]{3,2,1,0:T(4,128)(2,1)} %bitcast.23), channel_id=1, source_target_pairs={{0,2},{1,3},{2,0},{3,1},{4,6},{5,7},{6,4},{7,5},{8,10},{9,11},{10,... | collective-permute-start | bytes 98312 | tf_op jit(solution)/shard_map/ppermute | solution.py:248
  9.5 1.5 %copy.13 = bf16[1,4,64,2,8,128]{5,2,4,3,1,0:T(8,128)(2,1)S(1)} copy(bf16[1,4,64,2,8,128]{5,4,3,2,1,0:T(8,128)(2,1)} %param.12) | data formatting | bytes 2097152 | tf_op args[4]
  11.0 2.7 %replicas.4 = (bf16[1024,1024]{1,0:T(8,128)(2,1)S(1)}, f32[8,1024]{1,0:T(8,128)S(1)}) custom-call(s32[16]{0:T(128)S(1)} %fusion.9.slots, s32[1,4]{1,0:T(1,128)S(1)} %copy-done.3, f32[1,4]{1,0:T(1,128)S(1)} %copy-done.4, f32[1]{0:T(128)S(6)} %add.87.first_range, bf16[4,2,8,64,128]{4,3,2,1,0:T(8,128)(2,1)S(1)} %bitcast.13, bf16[1,512,256]{2,1,0:T(8,128)(2,1)S(1)} %copy-done, ...), custom_call_target="tpu_custom_call" | custom-call | flops 134217728 | bytes 8388608 | tf_op jit(solution)/shard_map/replicas/pallas_call | solution.py:139
  13.7 0.2 collective-permute-done.1
  13.9 0.1 pad_maximum_fusion.3.refs_4_
  14.0 0.9 %collective-permute-start.3 = (bf16[4,2,16,512]{3,2,1,0:T(8,128)(2,1)S(1)}, bf16[4,2,16,512]{3,2,1,0:T(8,128)(2,1)S(1)}, u32[]{:S(2)}, u32[]{:S(2)}) collective-permute-start(bf16[4,2,16,512]{3,2,1,0:T(8,128)(2,1)S(1)} %pad_maximum_fusion.3.refs_4_), channel_id=1, source_target_pairs={{0,9},{1,8},{2,11},{3,10},{4,13},{5,12},{6,15},{7,14},{8,1},{9,0},... | collective-permute-start | bytes 393224 | tf_op jit(solution)/shard_map/ppermute | solution.py:248
  14.9 1.5 %collective-permute-start.4 = (bf16[4,2,16,512]{3,2,1,0:T(8,128)(2,1)S(1)}, bf16[4,2,16,512]{3,2,1,0:T(8,128)(2,1)S(1)}, u32[]{:S(2)}, u32[]{:S(2)}) collective-permute-start(bf16[4,2,16,512]{3,2,1,0:T(8,128)(2,1)S(1)} %pad_maximum_fusion.3.refs_4_), channel_id=1, source_target_pairs={{0,8},{1,9},{2,10},{3,11},{4,12},{5,13},{6,14},{7,15},{8,0},{9,1},... | collective-permute-start | bytes 393224 | tf_op jit(solution)/shard_map/ppermute | solution.py:248
  16.4 1.2 %collective-permute-start.5 = (bf16[4,2,16,512]{3,2,1,0:T(8,128)(2,1)S(1)}, bf16[4,2,16,512]{3,2,1,0:T(8,128)(2,1)S(1)}, u32[]{:S(2)}, u32[]{:S(2)}) collective-permute-start(bf16[4,2,16,512]{3,2,1,0:T(8,128)(2,1)S(1)} %pad_maximum_fusion.3.refs_4_), channel_id=1, source_target_pairs={{0,1},{1,0},{2,3},{3,2},{4,5},{5,4},{6,7},{7,6},{8,9},{9,8},{10,11... | collective-permute-start | bytes 393224 | tf_op jit(solution)/shard_map/ppermute | solution.py:248
  17.6 2.7 %replicas.7 = (bf16[1024,1024]{1,0:T(8,128)(2,1)S(1)}, f32[8,1024]{1,0:T(8,128)S(1)}) custom-call(s32[16]{0:T(128)S(1)} %fusion.9.slots, s32[1,4]{1,0:T(1,128)S(1)} %copy-done.3, f32[1,4]{1,0:T(1,128)S(1)} %copy-done.4, f32[1]{0:T(128)S(6)} %add.87.first_range, bf16[4,2,8,64,128]{4,3,2,1,0:T(8,128)(2,1)S(1)} %bitcast.14, bf16[1,512,256]{2,1,0:T(8,128)(2,1)S(1)} %copy-done, ...), custom_call_target="tpu_custom_call" | custom-call | flops 134217728 | bytes 8388608 | tf_op jit(solution)/shard_map/replicas/pallas_call | solution.py:139
  20.3 2.7 %replicas.6 = (bf16[1024,1024]{1,0:T(8,128)(2,1)S(1)}, f32[8,1024]{1,0:T(8,128)S(1)}) custom-call(s32[16]{0:T(128)S(1)} %fusion.9.slots, s32[1,4]{1,0:T(1,128)S(1)} %copy-done.3, f32[1,4]{1,0:T(1,128)S(1)} %copy-done.4, f32[1]{0:T(128)S(6)} %add.87.first_range, bf16[4,2,8,64,128]{4,3,2,1,0:T(8,128)(2,1)S(1)} %bitcast.15, bf16[1,512,256]{2,1,0:T(8,128)(2,1)S(1)} %copy-done, ...), custom_call_target="tpu_custom_call" | custom-call | flops 134217728 | bytes 8388608 | tf_op jit(solution)/shard_map/replicas/pallas_call | solution.py:139
  23.0 2.7 %replicas.5 = (bf16[1024,1024]{1,0:T(8,128)(2,1)S(1)}, f32[8,1024]{1,0:T(8,128)S(1)}) custom-call(s32[16]{0:T(128)S(1)} %fusion.9.slots, s32[1,4]{1,0:T(1,128)S(1)} %copy-done.3, f32[1,4]{1,0:T(1,128)S(1)} %copy-done.4, f32[1]{0:T(128)S(6)} %add.87.first_range, bf16[4,2,8,64,128]{4,3,2,1,0:T(8,128)(2,1)S(1)} %bitcast.16, bf16[1,512,256]{2,1,0:T(8,128)(2,1)S(1)} %copy-done, ...), custom_call_target="tpu_custom_call" | custom-call | flops 134217728 | bytes 8388608 | tf_op jit(solution)/shard_map/replicas/pallas_call | solution.py:139
  25.8 2.3 %beams.1 = (f32[8,4,64,128]{3,2,1,0:T(8,128)S(1)}, bf16[8,4,64,128]{3,2,1,0:T(8,128)(2,1)S(1)}) custom-call(bf16[1024,1024]{1,0:T(8,128)(2,1)S(1)} %get-tuple-element.36.refs_0_, bf16[1024,1024]{1,0:T(8,128)(2,1)S(1)} %get-tuple-element.37.refs_1_, bf16[1024,1024]{1,0:T(8,128)(2,1)S(1)} %get-tuple-element.38.refs_2_, ...), custom_call_target="tpu_custom_call" | custom-call | flops 1073741824 | bytes 8388608 | tf_op jit(solution)/shard_map/beams/pallas_call | solution.py:184
  28.1 0.1 collective-permute-start.6
  28.2 0.1 reshape.25
  28.3 0.1 squeeze.16
  28.4 0.5 %collective-permute-start.7 = (f32[8,2,128]{2,1,0:T(2,128)S(1)}, f32[8,2,128]{2,1,0:T(2,128)S(1)}, u32[]{:S(2)}, u32[]{:S(2)}) collective-permute-start(f32[8,2,128]{2,1,0:T(2,128)S(1)} %squeeze.16), channel_id=1, source_target_pairs={{0,16},{16,0},{1,17},{17,1},{2,18},{18,2},{3,19},{19,3},{4,20},{20... | collective-permute-start | bytes 24584 | tf_op jit(solution)/shard_map/ppermute | solution.py:262
  28.9 0.1 squeeze.15
  29.0 1.1 %collective-permute-done.7 = f32[8,2,128]{2,1,0:T(2,128)S(1)} collective-permute-done((f32[8,2,128]{2,1,0:T(2,128)S(1)}, f32[8,2,128]{2,1,0:T(2,128)S(1)}, u32[]{:S(2)}, u32[]{:S(2)}) %collective-permute-start.7) | collective-permute-done | bytes 8224 | tf_op jit(solution)/shard_map/ppermute | solution.py:262
  30.1 0.2 fusion.12
  30.4 1.7 %collective-permute-start.10 = (bf16[2,260,128]{2,1,0:T(8,128)(2,1)S(1)}, bf16[2,260,128]{2,1,0:T(8,128)(2,1)S(1)}, u32[]{:S(2)}, u32[]{:S(2)}) collective-permute-start(bf16[2,260,128]{2,1,0:T(8,128)(2,1)S(1)} %pad_maximum_fusion.2), channel_id=1, source_target_pairs={{0,32},{32,0},{64,96},{96,64},{128,160},{160,128},{192,224},{224,1... | collective-permute-start | bytes 399368 | tf_op jit(solution)/shard_map/ppermute | solution.py:285
  32.1 2.3 %collective-permute-start.9 = (bf16[2,260,128]{2,1,0:T(8,128)(2,1)S(1)}, bf16[2,260,128]{2,1,0:T(8,128)(2,1)S(1)}, u32[]{:S(2)}, u32[]{:S(2)}) collective-permute-start(bf16[2,260,128]{2,1,0:T(8,128)(2,1)S(1)} %pad_maximum_fusion.1), channel_id=1, source_target_pairs={{0,96},{32,64},{64,32},{96,0},{128,224},{160,192},{192,160},{224,1... | collective-permute-start | bytes 399368 | tf_op jit(solution)/shard_map/ppermute | solution.py:285
  34.4 0.8 %collective-permute-start.8 = (bf16[2,260,128]{2,1,0:T(8,128)(2,1)S(1)}, bf16[2,260,128]{2,1,0:T(8,128)(2,1)S(1)}, u32[]{:S(2)}, u32[]{:S(2)}) collective-permute-start(bf16[2,260,128]{2,1,0:T(8,128)(2,1)S(1)} %pad_maximum_fusion), channel_id=1, source_target_pairs={{0,64},{32,96},{64,0},{96,32},{128,192},{160,224},{192,128},{224,1... | collective-permute-start | bytes 399368 | tf_op jit(solution)/shard_map/ppermute | solution.py:285
  35.2 0.9 %collective-permute-done.10 = bf16[2,260,128]{2,1,0:T(8,128)(2,1)S(1)} collective-permute-done((bf16[2,260,128]{2,1,0:T(8,128)(2,1)S(1)}, bf16[2,260,128]{2,1,0:T(8,128)(2,1)S(1)}, u32[]{:S(2)}, u32[]{:S(2)}) %collective-permute-start.10) | collective-permute-done | bytes 133152 | tf_op jit(solution)/shard_map/ppermute | solution.py:285
  36.2 5.5 %collective-permute-done.9 = bf16[2,260,128]{2,1,0:T(8,128)(2,1)S(1)} collective-permute-done((bf16[2,260,128]{2,1,0:T(8,128)(2,1)S(1)}, bf16[2,260,128]{2,1,0:T(8,128)(2,1)S(1)}, u32[]{:S(2)}, u32[]{:S(2)}) %collective-permute-start.9) | collective-permute-done | bytes 133152 | tf_op jit(solution)/shard_map/ppermute | solution.py:285
  41.7 0.1 slice_add_fusion
  41.8 2.2 %collective-permute-start.11 = (bf16[1,260,128]{2,1,0:T(8,128)(2,1)S(1)}, bf16[1,260,128]{2,1,0:T(8,128)(2,1)S(1)}, u32[]{:S(2)}, u32[]{:S(2)}) collective-permute-start(bf16[1,260,128]{2,1,0:T(8,128)(2,1)S(1)} %pad_maximum_fusion.4), channel_id=1, source_target_pairs={{0,128},{32,160},{64,192},{96,224},{128,0},{160,32},{192,64},{224,... | collective-permute-start | bytes 199688 | tf_op jit(solution)/shard_map/ppermute | solution.py:291
  44.1 3.7 %collective-permute-done.11 = bf16[1,260,128]{2,1,0:T(8,128)(2,1)S(1)} collective-permute-done((bf16[1,260,128]{2,1,0:T(8,128)(2,1)S(1)}, bf16[1,260,128]{2,1,0:T(8,128)(2,1)S(1)}, u32[]{:S(2)}, u32[]{:S(2)}) %collective-permute-start.11) | collective-permute-done | bytes 66592 | tf_op jit(solution)/shard_map/ppermute | solution.py:291
  47.7 0.1 fusion.1
  47.9 0.1 add.101
  48.0 0.1 add.105
  48.0 0.6 %log_multiply_fusion = f32[4,8,8]{2,1,0:T(8,128)} fusion(f32[4,8,8]{2,1,0:T(8,128)S(1)} %add.101, f32[4,8,8]{2,1,0:T(8,128)S(1)} %add.105), kind=kLoop, calls=%fused_computation.15 | loop fusion | flops 512 | bytes 3072 | tf_op jit(solution)/shard_map/mul | solution.py:295
  (46 shorter events, 0.4 us)
Async XLA Ops:
  0.0 13.9 %copy-start.5 = (bf16[1,4,2,4,512]{4,3,2,1,0:T(4,128)(2,1)S(1)}, bf16[1,4,2,4,512]{4,3,2,1,0:T(4,128)(2,1)}, u32[]{:S(2)}) copy-start(bf16[1,4,2,4,512]{4,3,2,1,0:T(4,128)(2,1)} %param.8) | copy-start | bytes 98308
  0.0 11.0 %copy-start.3 = (s32[1,4]{1,0:T(1,128)S(1)}, s32[1,4]{1,0:T(1,128)}, u32[]{:S(2)}) copy-start(s32[1,4]{1,0:T(1,128)} %counts.7) | copy-start | bytes 52
  0.0 11.0 %copy-start.4 = (f32[1,4]{1,0:T(1,128)S(1)}, f32[1,4]{1,0:T(1,128)}, u32[]{:S(2)}) copy-start(f32[1,4]{1,0:T(1,128)} %wave.7) | copy-start | bytes 52
  0.0 11.0 %copy-start = (bf16[1,512,256]{2,1,0:T(8,128)(2,1)S(1)}, bf16[1,512,256]{2,1,0:T(8,128)(2,1)}, u32[]{:S(2)}) copy-start(bf16[1,512,256]{2,1,0:T(8,128)(2,1)} %sensors.7) | copy-start | bytes 786436
  0.0 11.0 %copy-start.1 = (bf16[1,512]{1,0:T(2,128)(2,1)S(1)}, bf16[1,512]{1,0:T(2,128)(2,1)}, u32[]{:S(2)}) copy-start(bf16[1,512]{1,0:T(2,128)(2,1)} %curv.7) | copy-start | bytes 3076
  0.0 11.0 %copy-start.2 = (bf16[1,512]{1,0:T(2,128)(2,1)S(1)}, bf16[1,512]{1,0:T(2,128)(2,1)}, u32[]{:S(2)}) copy-start(bf16[1,512]{1,0:T(2,128)(2,1)} %offs.7) | copy-start | bytes 3076
  0.0 13.7 %collective-permute-start = (bf16[4,2,4,512]{3,2,1,0:T(4,128)(2,1)}, bf16[4,2,4,512]{3,2,1,0:T(4,128)(2,1)S(1)}, u32[]{:S(2)}, u32[]{:S(2)}) collective-permute-start(bf16[4,2,4,512]{3,2,1,0:T(4,128)(2,1)} %bitcast.21), channel_id=1, source_target_pairs={{0,4},{1,5},{2,6},{3,7},{4,0},{5,1},{6,2},{7,3},{8,12},{9,13},{10,... | collective-permute-start | bytes 98312 | tf_op jit(solution)/shard_map/ppermute | solution.py:248
  7.3 6.6 %collective-permute-start.1 = (bf16[4,2,4,512]{3,2,1,0:T(4,128)(2,1)}, bf16[4,2,4,512]{3,2,1,0:T(4,128)(2,1)S(1)}, u32[]{:S(2)}, u32[]{:S(2)}) collective-permute-start(bf16[4,2,4,512]{3,2,1,0:T(4,128)(2,1)} %bitcast.22), channel_id=1, source_target_pairs={{0,6},{1,7},{2,4},{3,5},{4,2},{5,3},{6,0},{7,1},{8,14},{9,15},{10,... | collective-permute-start | bytes 98312 | tf_op jit(solution)/shard_map/ppermute | solution.py:248
  7.3 6.6 %collective-permute-start.2 = (bf16[4,2,4,512]{3,2,1,0:T(4,128)(2,1)}, bf16[4,2,4,512]{3,2,1,0:T(4,128)(2,1)S(1)}, u32[]{:S(2)}, u32[]{:S(2)}) collective-permute-start(bf16[4,2,4,512]{3,2,1,0:T(4,128)(2,1)} %bitcast.23), channel_id=1, source_target_pairs={{0,2},{1,3},{2,0},{3,1},{4,6},{5,7},{6,4},{7,5},{8,10},{9,11},{10,... | collective-permute-start | bytes 98312 | tf_op jit(solution)/shard_map/ppermute | solution.py:248
  14.0 11.7 %collective-permute-start.3 = (bf16[4,2,16,512]{3,2,1,0:T(8,128)(2,1)S(1)}, bf16[4,2,16,512]{3,2,1,0:T(8,128)(2,1)S(1)}, u32[]{:S(2)}, u32[]{:S(2)}) collective-permute-start(bf16[4,2,16,512]{3,2,1,0:T(8,128)(2,1)S(1)} %pad_maximum_fusion.3.refs_4_), channel_id=1, source_target_pairs={{0,9},{1,8},{2,11},{3,10},{4,13},{5,12},{6,15},{7,14},{8,1},{9,0},... | collective-permute-start | bytes 393224 | tf_op jit(solution)/shard_map/ppermute | solution.py:248
  14.9 10.8 %collective-permute-start.4 = (bf16[4,2,16,512]{3,2,1,0:T(8,128)(2,1)S(1)}, bf16[4,2,16,512]{3,2,1,0:T(8,128)(2,1)S(1)}, u32[]{:S(2)}, u32[]{:S(2)}) collective-permute-start(bf16[4,2,16,512]{3,2,1,0:T(8,128)(2,1)S(1)} %pad_maximum_fusion.3.refs_4_), channel_id=1, source_target_pairs={{0,8},{1,9},{2,10},{3,11},{4,12},{5,13},{6,14},{7,15},{8,0},{9,1},... | collective-permute-start | bytes 393224 | tf_op jit(solution)/shard_map/ppermute | solution.py:248
  16.4 9.4 %collective-permute-start.5 = (bf16[4,2,16,512]{3,2,1,0:T(8,128)(2,1)S(1)}, bf16[4,2,16,512]{3,2,1,0:T(8,128)(2,1)S(1)}, u32[]{:S(2)}, u32[]{:S(2)}) collective-permute-start(bf16[4,2,16,512]{3,2,1,0:T(8,128)(2,1)S(1)} %pad_maximum_fusion.3.refs_4_), channel_id=1, source_target_pairs={{0,1},{1,0},{2,3},{3,2},{4,5},{5,4},{6,7},{7,6},{8,9},{9,8},{10,11... | collective-permute-start | bytes 393224 | tf_op jit(solution)/shard_map/ppermute | solution.py:248
  28.1 2.0 %collective-permute-start.6 = (bf16[8,4,64,128]{3,2,1,0:T(8,128)(2,1)S(1)}, bf16[8,4,64,128]{3,2,1,0:T(8,128)(2,1)S(1)}, u32[]{:S(2)}, u32[]{:S(2)}) collective-permute-start(bf16[8,4,64,128]{3,2,1,0:T(8,128)(2,1)S(1)} %get-tuple-element.44), channel_id=1, source_target_pairs={{0,16},{16,0},{1,17},{17,1},{2,18},{18,2},{3,19},{19,3},{4,20},{20... | collective-permute-start | bytes 1572872 | tf_op jit(solution)/shard_map/ppermute | solution.py:266
  28.4 1.7 %collective-permute-start.7 = (f32[8,2,128]{2,1,0:T(2,128)S(1)}, f32[8,2,128]{2,1,0:T(2,128)S(1)}, u32[]{:S(2)}, u32[]{:S(2)}) collective-permute-start(f32[8,2,128]{2,1,0:T(2,128)S(1)} %squeeze.16), channel_id=1, source_target_pairs={{0,16},{16,0},{1,17},{17,1},{2,18},{18,2},{3,19},{19,3},{4,20},{20... | collective-permute-start | bytes 24584 | tf_op jit(solution)/shard_map/ppermute | solution.py:262
  30.4 5.7 %collective-permute-start.10 = (bf16[2,260,128]{2,1,0:T(8,128)(2,1)S(1)}, bf16[2,260,128]{2,1,0:T(8,128)(2,1)S(1)}, u32[]{:S(2)}, u32[]{:S(2)}) collective-permute-start(bf16[2,260,128]{2,1,0:T(8,128)(2,1)S(1)} %pad_maximum_fusion.2), channel_id=1, source_target_pairs={{0,32},{32,0},{64,96},{96,64},{128,160},{160,128},{192,224},{224,1... | collective-permute-start | bytes 399368 | tf_op jit(solution)/shard_map/ppermute | solution.py:285
  32.1 9.5 %collective-permute-start.9 = (bf16[2,260,128]{2,1,0:T(8,128)(2,1)S(1)}, bf16[2,260,128]{2,1,0:T(8,128)(2,1)S(1)}, u32[]{:S(2)}, u32[]{:S(2)}) collective-permute-start(bf16[2,260,128]{2,1,0:T(8,128)(2,1)S(1)} %pad_maximum_fusion.1), channel_id=1, source_target_pairs={{0,96},{32,64},{64,32},{96,0},{128,224},{160,192},{192,160},{224,1... | collective-permute-start | bytes 399368 | tf_op jit(solution)/shard_map/ppermute | solution.py:285
  34.4 7.3 %collective-permute-start.8 = (bf16[2,260,128]{2,1,0:T(8,128)(2,1)S(1)}, bf16[2,260,128]{2,1,0:T(8,128)(2,1)S(1)}, u32[]{:S(2)}, u32[]{:S(2)}) collective-permute-start(bf16[2,260,128]{2,1,0:T(8,128)(2,1)S(1)} %pad_maximum_fusion), channel_id=1, source_target_pairs={{0,64},{32,96},{64,0},{96,32},{128,192},{160,224},{192,128},{224,1... | collective-permute-start | bytes 399368 | tf_op jit(solution)/shard_map/ppermute | solution.py:285
  41.8 5.9 %collective-permute-start.11 = (bf16[1,260,128]{2,1,0:T(8,128)(2,1)S(1)}, bf16[1,260,128]{2,1,0:T(8,128)(2,1)S(1)}, u32[]{:S(2)}, u32[]{:S(2)}) collective-permute-start(bf16[1,260,128]{2,1,0:T(8,128)(2,1)S(1)} %pad_maximum_fusion.4), channel_id=1, source_target_pairs={{0,128},{32,160},{64,192},{96,224},{128,0},{160,32},{192,64},{224,... | collective-permute-start | bytes 199688 | tf_op jit(solution)/shard_map/ppermute | solution.py:291

commit v3 on v2

--- a/solution.py
+++ b/solution.py
@@ -48,7 +48,7 @@
     offs,
     *rest,
 ):
-    out, energy, a32, sums, now_c, now_s, old_c, old_s, twice, esum, placed = rest
+    out, energy, a32, sums, now_c, now_s, old_c, old_s, twice, esum = rest
     modes = cm.shape[3]
     rows = cm.shape[2]
     depth = cm.shape[4]
@@ -91,17 +91,15 @@
 
     def one_pair(pair, carry):
         here = pl.ds(pl.multiple_of(pair * 2 * Z0, 2 * Z0), 2 * Z0)
-        tiles = phones // 128
-        group = 4
-        for lead in range(0, tiles, group):
-            spans = [slice(i * 128, (i + 1) * 128) for i in range(lead, lead + group)]
+        if True:
+            spans = [slice(i, i + 128) for i in range(0, phones, 128)]
             turns = [(now_c[here, at], now_s[here, at]) for at in spans]
             before = [(old_c[here, at], old_s[here, at]) for at in spans]
             steps = [twice[here, at] for at in spans]
             for block in range(blocks):
                 first = pl.multiple_of(block * tile_rows + pair * 2 * Z0, 2 * Z0)
                 to = pl.multiple_of(slots[block] * tile_rows + pair * 2 * Z0, 2 * Z0)
-                power = jnp.zeros((2 * Z0, 128), f32) if lead == 0 else esum[pl.ds(first, 2 * Z0), :]
+                power = jnp.zeros((2 * Z0, 128), f32)
                 for i, at in enumerate(spans):
                     c, s = turns[i]
                     m0 = sums[pl.ds(first, 2 * Z0), at]
@@ -113,20 +111,13 @@
                     power = power + (m0 * m0 + m1 * m1)
                     turns[i] = (steps[i] * c - before[i][0], steps[i] * s - before[i][1])
                     before[i] = (c, s)
-                esum[pl.ds(first, 2 * Z0), :] = power
+                esum[pl.ds(to, 2 * Z0), :] = power
         return carry
 
     lax.fori_loop(0, rows // 2, one_pair, 0, unroll=True)
-    for block in range(blocks):
-        to = pl.multiple_of(slots[block] * tile_rows, tile_rows)
-        placed[pl.ds(to, tile_rows), :] = esum[block * tile_rows : (block + 1) * tile_rows, :]
-    total = placed[...]
-    high = total.astype(bf16)
-    rest_of = (total - high.astype(f32)).astype(bf16)
-    ones = jnp.ones((8, 128), bf16)
-    energy[...] = lax.dot_general(
-        ones, high, NT, preferred_element_type=f32
-    ) + lax.dot_general(ones, rest_of, NT, preferred_element_type=f32)
+    for i in range(0, half, 128):
+        line = jnp.sum(esum[i : i + 128, :].T, axis=0, keepdims=True)
+        energy[:, i : i + 128] = jnp.broadcast_to(line, (8, 128))
 
 
 def replicas(bin_index, slots, counts, wave, first_range, cm, sensors, curv, offs):
@@ -148,7 +139,7 @@
             pltpu.VMEM((2, blocks, rows, Z0, modes), f32),
             pltpu.VMEM((2 * cells, phones), f32),
             *[pltpu.VMEM((rows * Z0, phones), f32)] * 5,
-            *[pltpu.VMEM((cells, 128), f32)] * 2,
+            pltpu.VMEM((cells, 128), f32),
         ],
         compiler_params=pltpu.CompilerParams(vmem_limit_bytes=24 * 2**20),
         cost_estimate=pl.CostEstimate(
@@ -171,7 +162,7 @@
         kept = lax.dot_general(w[:half], signal, NT, preferred_element_type=f32)
         sent = lax.dot_general(w[half:], signal, NT, preferred_element_type=f32)
         keep[:, b] = kept.reshape(keep.shape[0], keep.shape[2], keep.shape[3])
-        send[:, b] = sent.reshape(send.shape[0], send.shape[2], send.shape[3]).astype(bf16)
+        send[:, b] = sent.reshape(send.shape[0], send.shape[2], send.shape[3])
 
 
 def beams(ws, pieces):
@@ -185,7 +176,7 @@
         functools.partial(beam_kernel, bins),
         in_specs=[vmem] * (bins + len(pieces)),
         out_specs=[vmem] * 2,
-        out_shape=[jax.ShapeDtypeStruct(out, f32), jax.ShapeDtypeStruct(out, bf16)],
+        out_shape=[jax.ShapeDtypeStruct(out, f32)] * 2,
         compiler_params=pltpu.CompilerParams(vmem_limit_bytes=24 * 2**20),
         cost_estimate=pl.CostEstimate(
             flops=2 * bins * cells * depth * looks,
@@ -264,7 +255,7 @@
     keep, send = beams(ws, pieces)
     swap = [(0, 1), (1, 0)]
     got = lax.ppermute(send, "sens", swap)
-    beam = keep + got.astype(f32)
+    beam = keep + got
     owners, looks = beam.shape[0], beam.shape[3]
     beam = beam.reshape(owners, -1, looks)
     cells, lines = beam.shape[1], energy.shape[1]

time: 48.8 us -> 49.5 us (1.014)
  waiting for transfers between devices: 11.4 us -> 12.1 us
    ppermute x1, waiting for transfers between devices: 1.08 us -> 1.8 us  [local(): energy = energy[0] + lax.ppermute(energy[1], 'sens', [(0, 1), (1, 0)])]
where the time goes in v3:
time: 49.5 us; the launch traced here: 49.4 us
  starting transfers between devices  19.9 us (40%)
  Pallas kernels  13.1 us (26%)
  waiting for transfers between devices  12.1 us (24%)
  local copies, waits for them, and re-layouts  2.03 us (4%)
  other arithmetic  1.3 us (3%)
  between operations  0.98 us (2%)
    ppermute x6, starting transfers between devices, from_cell(): return lax.ppermute(piece, 'cell', [(i, i ^ flip) for i in range(16)])  12.3 us
    pallas_call x4, Pallas kernels, replicas(): pl.pallas_call(functools.partial(replica_kernel, bin_index), in_specs=[sm...  10.8 us
    ppermute x3, waiting for transfers between devices, local(): lax.ppermute(sent(slice(2 * k, 2 * k + 2)), 'sub', [(i, i ^ k) for i in r...  6.41 us
    ppermute x3, starting transfers between devices, local(): lax.ppermute(sent(slice(2 * k, 2 * k + 2)), 'sub', [(i, i ^ k) for i in r...  4.73 us
    ppermute x1, waiting for transfers between devices, local(): got = lax.ppermute(sent(slice(1, 2)), 'sub', [(i, i ^ 4) for i in range(8)])  3.66 us
    pallas_call x1, Pallas kernels, beams(): pl.pallas_call(functools.partial(beam_kernel, bins), in_specs=[vmem] * (b...  2.33 us
    ppermute x1, starting transfers between devices, local(): got = lax.ppermute(sent(slice(1, 2)), 'sub', [(i, i ^ 4) for i in range(8)])  2.22 us
    ppermute x1, waiting for transfers between devices, local(): energy = energy[0] + lax.ppermute(energy[1], 'sens', [(0, 1), (1, 0)])  1.8 us
  transfers between devices with their start and end apart: 12, of which 5 were waited for; matrix products, arithmetic and copies ran while one was open for 4% of the time, Pallas kernels for 22%

profile of v3, /device:TPU:2, one launch (start us, length us, event | category | flops | bytes accessed | tf_op | source)
XLA Modules:
  0.0 49.4 jit_solution(3084460683860527583)
XLA Ops:
  0.0 7.3 %collective-permute-start = (bf16[4,2,4,512]{3,2,1,0:T(4,128)(2,1)}, bf16[4,2,4,512]{3,2,1,0:T(4,128)(2,1)S(1)}, u32[]{:S(2)}, u32[]{:S(2)}) collective-permute-start(bf16[4,2,4,512]{3,2,1,0:T(4,128)(2,1)} %bitcast.21), channel_id=1, source_target_pairs={{0,4},{1,5},{2,6},{3,7},{4,0},{5,1},{6,2},{7,3},{8,12},{9,13},{10,... | collective-permute-start | bytes 98312 | tf_op jit(solution)/shard_map/ppermute | solution.py:239
  7.3 1.5 %collective-permute-start.2 = (bf16[4,2,4,512]{3,2,1,0:T(4,128)(2,1)}, bf16[4,2,4,512]{3,2,1,0:T(4,128)(2,1)S(1)}, u32[]{:S(2)}, u32[]{:S(2)}) collective-permute-start(bf16[4,2,4,512]{3,2,1,0:T(4,128)(2,1)} %bitcast.23), channel_id=1, source_target_pairs={{0,2},{1,3},{2,0},{3,1},{4,6},{5,7},{6,4},{7,5},{8,10},{9,11},{10,... | collective-permute-start | bytes 98312 | tf_op jit(solution)/shard_map/ppermute | solution.py:239
  9.5 1.5 %copy.13 = bf16[1,4,64,2,8,128]{5,2,4,3,1,0:T(8,128)(2,1)S(1)} copy(bf16[1,4,64,2,8,128]{5,4,3,2,1,0:T(8,128)(2,1)} %param.12) | data formatting | bytes 2097152 | tf_op args[4]
  11.0 2.7 %replicas.4 = (bf16[1024,1024]{1,0:T(8,128)(2,1)S(1)}, f32[8,1024]{1,0:T(8,128)S(1)}) custom-call(s32[16]{0:T(128)S(1)} %fusion.9.slots, s32[1,4]{1,0:T(1,128)S(1)} %copy-done.3, f32[1,4]{1,0:T(1,128)S(1)} %copy-done.4, f32[1]{0:T(128)S(6)} %add.87.first_range, bf16[4,2,8,64,128]{4,3,2,1,0:T(8,128)(2,1)S(1)} %bitcast.13, bf16[1,512,256]{2,1,0:T(8,128)(2,1)S(1)} %copy-done, ...), custom_call_target="tpu_custom_call" | custom-call | flops 134217728 | bytes 8388608 | tf_op jit(solution)/shard_map/replicas/pallas_call | solution.py:130
  13.7 0.2 collective-permute-done.1
  13.9 0.1 pad_maximum_fusion.3.refs_4_
  14.0 0.9 %collective-permute-start.3 = (bf16[4,2,16,512]{3,2,1,0:T(8,128)(2,1)S(1)}, bf16[4,2,16,512]{3,2,1,0:T(8,128)(2,1)S(1)}, u32[]{:S(2)}, u32[]{:S(2)}) collective-permute-start(bf16[4,2,16,512]{3,2,1,0:T(8,128)(2,1)S(1)} %pad_maximum_fusion.3.refs_4_), channel_id=1, source_target_pairs={{0,9},{1,8},{2,11},{3,10},{4,13},{5,12},{6,15},{7,14},{8,1},{9,0},... | collective-permute-start | bytes 393224 | tf_op jit(solution)/shard_map/ppermute | solution.py:239
  14.9 1.5 %collective-permute-start.4 = (bf16[4,2,16,512]{3,2,1,0:T(8,128)(2,1)S(1)}, bf16[4,2,16,512]{3,2,1,0:T(8,128)(2,1)S(1)}, u32[]{:S(2)}, u32[]{:S(2)}) collective-permute-start(bf16[4,2,16,512]{3,2,1,0:T(8,128)(2,1)S(1)} %pad_maximum_fusion.3.refs_4_), channel_id=1, source_target_pairs={{0,8},{1,9},{2,10},{3,11},{4,12},{5,13},{6,14},{7,15},{8,0},{9,1},... | collective-permute-start | bytes 393224 | tf_op jit(solution)/shard_map/ppermute | solution.py:239
  16.4 1.2 %collective-permute-start.5 = (bf16[4,2,16,512]{3,2,1,0:T(8,128)(2,1)S(1)}, bf16[4,2,16,512]{3,2,1,0:T(8,128)(2,1)S(1)}, u32[]{:S(2)}, u32[]{:S(2)}) collective-permute-start(bf16[4,2,16,512]{3,2,1,0:T(8,128)(2,1)S(1)} %pad_maximum_fusion.3.refs_4_), channel_id=1, source_target_pairs={{0,1},{1,0},{2,3},{3,2},{4,5},{5,4},{6,7},{7,6},{8,9},{9,8},{10,11... | collective-permute-start | bytes 393224 | tf_op jit(solution)/shard_map/ppermute | solution.py:239
  17.6 2.7 %replicas.7 = (bf16[1024,1024]{1,0:T(8,128)(2,1)S(1)}, f32[8,1024]{1,0:T(8,128)S(1)}) custom-call(s32[16]{0:T(128)S(1)} %fusion.9.slots, s32[1,4]{1,0:T(1,128)S(1)} %copy-done.3, f32[1,4]{1,0:T(1,128)S(1)} %copy-done.4, f32[1]{0:T(128)S(6)} %add.87.first_range, bf16[4,2,8,64,128]{4,3,2,1,0:T(8,128)(2,1)S(1)} %bitcast.14, bf16[1,512,256]{2,1,0:T(8,128)(2,1)S(1)} %copy-done, ...), custom_call_target="tpu_custom_call" | custom-call | flops 134217728 | bytes 8388608 | tf_op jit(solution)/shard_map/replicas/pallas_call | solution.py:130
  20.3 2.7 %replicas.6 = (bf16[1024,1024]{1,0:T(8,128)(2,1)S(1)}, f32[8,1024]{1,0:T(8,128)S(1)}) custom-call(s32[16]{0:T(128)S(1)} %fusion.9.slots, s32[1,4]{1,0:T(1,128)S(1)} %copy-done.3, f32[1,4]{1,0:T(1,128)S(1)} %copy-done.4, f32[1]{0:T(128)S(6)} %add.87.first_range, bf16[4,2,8,64,128]{4,3,2,1,0:T(8,128)(2,1)S(1)} %bitcast.15, bf16[1,512,256]{2,1,0:T(8,128)(2,1)S(1)} %copy-done, ...), custom_call_target="tpu_custom_call" | custom-call | flops 134217728 | bytes 8388608 | tf_op jit(solution)/shard_map/replicas/pallas_call | solution.py:130
  23.0 2.7 %replicas.5 = (bf16[1024,1024]{1,0:T(8,128)(2,1)S(1)}, f32[8,1024]{1,0:T(8,128)S(1)}) custom-call(s32[16]{0:T(128)S(1)} %fusion.9.slots, s32[1,4]{1,0:T(1,128)S(1)} %copy-done.3, f32[1,4]{1,0:T(1,128)S(1)} %copy-done.4, f32[1]{0:T(128)S(6)} %add.87.first_range, bf16[4,2,8,64,128]{4,3,2,1,0:T(8,128)(2,1)S(1)} %bitcast.16, bf16[1,512,256]{2,1,0:T(8,128)(2,1)S(1)} %copy-done, ...), custom_call_target="tpu_custom_call" | custom-call | flops 134217728 | bytes 8388608 | tf_op jit(solution)/shard_map/replicas/pallas_call | solution.py:130
  25.7 2.3 %beams.1 = (f32[8,4,64,128]{3,2,1,0:T(8,128)S(1)}, f32[8,4,64,128]{3,2,1,0:T(8,128)S(1)}) custom-call(bf16[1024,1024]{1,0:T(8,128)(2,1)S(1)} %get-tuple-element.36.refs_0_, bf16[1024,1024]{1,0:T(8,128)(2,1)S(1)} %get-tuple-element.37.refs_1_, bf16[1024,1024]{1,0:T(8,128)(2,1)S(1)} %get-tuple-element.38.refs_2_, ...), custom_call_target="tpu_custom_call" | custom-call | flops 1073741824 | bytes 8388608 | tf_op jit(solution)/shard_map/beams/pallas_call | solution.py:175
  28.1 0.1 collective-permute-start.6
  28.2 0.1 reshape.25
  28.4 0.1 squeeze.16
  28.4 0.5 %collective-permute-start.7 = (f32[8,2,128]{2,1,0:T(2,128)S(1)}, f32[8,2,128]{2,1,0:T(2,128)S(1)}, u32[]{:S(2)}, u32[]{:S(2)}) collective-permute-start(f32[8,2,128]{2,1,0:T(2,128)S(1)} %squeeze.16), channel_id=1, source_target_pairs={{0,16},{16,0},{1,17},{17,1},{2,18},{18,2},{3,19},{19,3},{4,20},{20... | collective-permute-start | bytes 24584 | tf_op jit(solution)/shard_map/ppermute | solution.py:253
  28.9 0.1 squeeze.15
  29.0 1.8 %collective-permute-done.7 = f32[8,2,128]{2,1,0:T(2,128)S(1)} collective-permute-done((f32[8,2,128]{2,1,0:T(2,128)S(1)}, f32[8,2,128]{2,1,0:T(2,128)S(1)}, u32[]{:S(2)}, u32[]{:S(2)}) %collective-permute-start.7) | collective-permute-done | bytes 8224 | tf_op jit(solution)/shard_map/ppermute | solution.py:253
  30.9 0.2 fusion.12
  31.1 1.7 %collective-permute-start.10 = (bf16[2,260,128]{2,1,0:T(8,128)(2,1)S(1)}, bf16[2,260,128]{2,1,0:T(8,128)(2,1)S(1)}, u32[]{:S(2)}, u32[]{:S(2)}) collective-permute-start(bf16[2,260,128]{2,1,0:T(8,128)(2,1)S(1)} %pad_maximum_fusion.2), channel_id=1, source_target_pairs={{0,32},{32,0},{64,96},{96,64},{128,160},{160,128},{192,224},{224,1... | collective-permute-start | bytes 399368 | tf_op jit(solution)/shard_map/ppermute | solution.py:276
  32.8 2.3 %collective-permute-start.9 = (bf16[2,260,128]{2,1,0:T(8,128)(2,1)S(1)}, bf16[2,260,128]{2,1,0:T(8,128)(2,1)S(1)}, u32[]{:S(2)}, u32[]{:S(2)}) collective-permute-start(bf16[2,260,128]{2,1,0:T(8,128)(2,1)S(1)} %pad_maximum_fusion.1), channel_id=1, source_target_pairs={{0,96},{32,64},{64,32},{96,0},{128,224},{160,192},{192,160},{224,1... | collective-permute-start | bytes 399368 | tf_op jit(solution)/shard_map/ppermute | solution.py:276
  35.0 0.8 %collective-permute-start.8 = (bf16[2,260,128]{2,1,0:T(8,128)(2,1)S(1)}, bf16[2,260,128]{2,1,0:T(8,128)(2,1)S(1)}, u32[]{:S(2)}, u32[]{:S(2)}) collective-permute-start(bf16[2,260,128]{2,1,0:T(8,128)(2,1)S(1)} %pad_maximum_fusion), channel_id=1, source_target_pairs={{0,64},{32,96},{64,0},{96,32},{128,192},{160,224},{192,128},{224,1... | collective-permute-start | bytes 399368 | tf_op jit(solution)/shard_map/ppermute | solution.py:276
  35.9 0.9 %collective-permute-done.10 = bf16[2,260,128]{2,1,0:T(8,128)(2,1)S(1)} collective-permute-done((bf16[2,260,128]{2,1,0:T(8,128)(2,1)S(1)}, bf16[2,260,128]{2,1,0:T(8,128)(2,1)S(1)}, u32[]{:S(2)}, u32[]{:S(2)}) %collective-permute-start.10) | collective-permute-done | bytes 133152 | tf_op jit(solution)/shard_map/ppermute | solution.py:276
  36.8 5.5 %collective-permute-done.9 = bf16[2,260,128]{2,1,0:T(8,128)(2,1)S(1)} collective-permute-done((bf16[2,260,128]{2,1,0:T(8,128)(2,1)S(1)}, bf16[2,260,128]{2,1,0:T(8,128)(2,1)S(1)}, u32[]{:S(2)}, u32[]{:S(2)}) %collective-permute-start.9) | collective-permute-done | bytes 133152 | tf_op jit(solution)/shard_map/ppermute | solution.py:276
  42.4 0.1 slice_add_fusion
  42.5 2.2 %collective-permute-start.11 = (bf16[1,260,128]{2,1,0:T(8,128)(2,1)S(1)}, bf16[1,260,128]{2,1,0:T(8,128)(2,1)S(1)}, u32[]{:S(2)}, u32[]{:S(2)}) collective-permute-start(bf16[1,260,128]{2,1,0:T(8,128)(2,1)S(1)} %pad_maximum_fusion.4), channel_id=1, source_target_pairs={{0,128},{32,160},{64,192},{96,224},{128,0},{160,32},{192,64},{224,... | collective-permute-start | bytes 199688 | tf_op jit(solution)/shard_map/ppermute | solution.py:282
  44.7 3.7 %collective-permute-done.11 = bf16[1,260,128]{2,1,0:T(8,128)(2,1)S(1)} collective-permute-done((bf16[1,260,128]{2,1,0:T(8,128)(2,1)S(1)}, bf16[1,260,128]{2,1,0:T(8,128)(2,1)S(1)}, u32[]{:S(2)}, u32[]{:S(2)}) %collective-permute-start.11) | collective-permute-done | bytes 66592 | tf_op jit(solution)/shard_map/ppermute | solution.py:282
  48.4 0.1 fusion.1
  48.5 0.1 add.101
  48.6 0.1 add.105
  48.7 0.6 %log_multiply_fusion = f32[4,8,8]{2,1,0:T(8,128)} fusion(f32[4,8,8]{2,1,0:T(8,128)S(1)} %add.101, f32[4,8,8]{2,1,0:T(8,128)S(1)} %add.105), kind=kLoop, calls=%fused_computation.14 | loop fusion | flops 512 | bytes 3072 | tf_op jit(solution)/shard_map/mul | solution.py:286
  (46 shorter events, 0.3 us)
Async XLA Ops:
  0.0 13.9 %copy-start.5 = (bf16[1,4,2,4,512]{4,3,2,1,0:T(4,128)(2,1)S(1)}, bf16[1,4,2,4,512]{4,3,2,1,0:T(4,128)(2,1)}, u32[]{:S(2)}) copy-start(bf16[1,4,2,4,512]{4,3,2,1,0:T(4,128)(2,1)} %param.8) | copy-start | bytes 98308
  0.0 11.0 %copy-start.3 = (s32[1,4]{1,0:T(1,128)S(1)}, s32[1,4]{1,0:T(1,128)}, u32[]{:S(2)}) copy-start(s32[1,4]{1,0:T(1,128)} %counts.7) | copy-start | bytes 52
  0.0 11.0 %copy-start.4 = (f32[1,4]{1,0:T(1,128)S(1)}, f32[1,4]{1,0:T(1,128)}, u32[]{:S(2)}) copy-start(f32[1,4]{1,0:T(1,128)} %wave.7) | copy-start | bytes 52
  0.0 11.0 %copy-start = (bf16[1,512,256]{2,1,0:T(8,128)(2,1)S(1)}, bf16[1,512,256]{2,1,0:T(8,128)(2,1)}, u32[]{:S(2)}) copy-start(bf16[1,512,256]{2,1,0:T(8,128)(2,1)} %sensors.7) | copy-start | bytes 786436
  0.0 11.0 %copy-start.1 = (bf16[1,512]{1,0:T(2,128)(2,1)S(1)}, bf16[1,512]{1,0:T(2,128)(2,1)}, u32[]{:S(2)}) copy-start(bf16[1,512]{1,0:T(2,128)(2,1)} %curv.7) | copy-start | bytes 3076
  0.0 11.0 %copy-start.2 = (bf16[1,512]{1,0:T(2,128)(2,1)S(1)}, bf16[1,512]{1,0:T(2,128)(2,1)}, u32[]{:S(2)}) copy-start(bf16[1,512]{1,0:T(2,128)(2,1)} %offs.7) | copy-start | bytes 3076
  0.0 13.7 %collective-permute-start = (bf16[4,2,4,512]{3,2,1,0:T(4,128)(2,1)}, bf16[4,2,4,512]{3,2,1,0:T(4,128)(2,1)S(1)}, u32[]{:S(2)}, u32[]{:S(2)}) collective-permute-start(bf16[4,2,4,512]{3,2,1,0:T(4,128)(2,1)} %bitcast.21), channel_id=1, source_target_pairs={{0,4},{1,5},{2,6},{3,7},{4,0},{5,1},{6,2},{7,3},{8,12},{9,13},{10,... | collective-permute-start | bytes 98312 | tf_op jit(solution)/shard_map/ppermute | solution.py:239
  7.3 6.6 %collective-permute-start.1 = (bf16[4,2,4,512]{3,2,1,0:T(4,128)(2,1)}, bf16[4,2,4,512]{3,2,1,0:T(4,128)(2,1)S(1)}, u32[]{:S(2)}, u32[]{:S(2)}) collective-permute-start(bf16[4,2,4,512]{3,2,1,0:T(4,128)(2,1)} %bitcast.22), channel_id=1, source_target_pairs={{0,6},{1,7},{2,4},{3,5},{4,2},{5,3},{6,0},{7,1},{8,14},{9,15},{10,... | collective-permute-start | bytes 98312 | tf_op jit(solution)/shard_map/ppermute | solution.py:239
  7.3 6.6 %collective-permute-start.2 = (bf16[4,2,4,512]{3,2,1,0:T(4,128)(2,1)}, bf16[4,2,4,512]{3,2,1,0:T(4,128)(2,1)S(1)}, u32[]{:S(2)}, u32[]{:S(2)}) collective-permute-start(bf16[4,2,4,512]{3,2,1,0:T(4,128)(2,1)} %bitcast.23), channel_id=1, source_target_pairs={{0,2},{1,3},{2,0},{3,1},{4,6},{5,7},{6,4},{7,5},{8,10},{9,11},{10,... | collective-permute-start | bytes 98312 | tf_op jit(solution)/shard_map/ppermute | solution.py:239
  14.0 11.7 %collective-permute-start.3 = (bf16[4,2,16,512]{3,2,1,0:T(8,128)(2,1)S(1)}, bf16[4,2,16,512]{3,2,1,0:T(8,128)(2,1)S(1)}, u32[]{:S(2)}, u32[]{:S(2)}) collective-permute-start(bf16[4,2,16,512]{3,2,1,0:T(8,128)(2,1)S(1)} %pad_maximum_fusion.3.refs_4_), channel_id=1, source_target_pairs={{0,9},{1,8},{2,11},{3,10},{4,13},{5,12},{6,15},{7,14},{8,1},{9,0},... | collective-permute-start | bytes 393224 | tf_op jit(solution)/shard_map/ppermute | solution.py:239
  14.9 10.8 %collective-permute-start.4 = (bf16[4,2,16,512]{3,2,1,0:T(8,128)(2,1)S(1)}, bf16[4,2,16,512]{3,2,1,0:T(8,128)(2,1)S(1)}, u32[]{:S(2)}, u32[]{:S(2)}) collective-permute-start(bf16[4,2,16,512]{3,2,1,0:T(8,128)(2,1)S(1)} %pad_maximum_fusion.3.refs_4_), channel_id=1, source_target_pairs={{0,8},{1,9},{2,10},{3,11},{4,12},{5,13},{6,14},{7,15},{8,0},{9,1},... | collective-permute-start | bytes 393224 | tf_op jit(solution)/shard_map/ppermute | solution.py:239
  16.4 9.3 %collective-permute-start.5 = (bf16[4,2,16,512]{3,2,1,0:T(8,128)(2,1)S(1)}, bf16[4,2,16,512]{3,2,1,0:T(8,128)(2,1)S(1)}, u32[]{:S(2)}, u32[]{:S(2)}) collective-permute-start(bf16[4,2,16,512]{3,2,1,0:T(8,128)(2,1)S(1)} %pad_maximum_fusion.3.refs_4_), channel_id=1, source_target_pairs={{0,1},{1,0},{2,3},{3,2},{4,5},{5,4},{6,7},{7,6},{8,9},{9,8},{10,11... | collective-permute-start | bytes 393224 | tf_op jit(solution)/shard_map/ppermute | solution.py:239
  28.1 2.8 %collective-permute-start.6 = (f32[8,4,64,128]{3,2,1,0:T(8,128)S(1)}, f32[8,4,64,128]{3,2,1,0:T(8,128)S(1)}, u32[]{:S(2)}, u32[]{:S(2)}) collective-permute-start(f32[8,4,64,128]{3,2,1,0:T(8,128)S(1)} %get-tuple-element.44), channel_id=1, source_target_pairs={{0,16},{16,0},{1,17},{17,1},{2,18},{18,2},{3,19},{19,3},{4,20},{20... | collective-permute-start | bytes 3145736 | tf_op jit(solution)/shard_map/ppermute | solution.py:257
  28.4 2.4 %collective-permute-start.7 = (f32[8,2,128]{2,1,0:T(2,128)S(1)}, f32[8,2,128]{2,1,0:T(2,128)S(1)}, u32[]{:S(2)}, u32[]{:S(2)}) collective-permute-start(f32[8,2,128]{2,1,0:T(2,128)S(1)} %squeeze.16), channel_id=1, source_target_pairs={{0,16},{16,0},{1,17},{17,1},{2,18},{18,2},{3,19},{19,3},{4,20},{20... | collective-permute-start | bytes 24584 | tf_op jit(solution)/shard_map/ppermute | solution.py:253
  31.1 5.7 %collective-permute-start.10 = (bf16[2,260,128]{2,1,0:T(8,128)(2,1)S(1)}, bf16[2,260,128]{2,1,0:T(8,128)(2,1)S(1)}, u32[]{:S(2)}, u32[]{:S(2)}) collective-permute-start(bf16[2,260,128]{2,1,0:T(8,128)(2,1)S(1)} %pad_maximum_fusion.2), channel_id=1, source_target_pairs={{0,32},{32,0},{64,96},{96,64},{128,160},{160,128},{192,224},{224,1... | collective-permute-start | bytes 399368 | tf_op jit(solution)/shard_map/ppermute | solution.py:276
  32.8 9.5 %collective-permute-start.9 = (bf16[2,260,128]{2,1,0:T(8,128)(2,1)S(1)}, bf16[2,260,128]{2,1,0:T(8,128)(2,1)S(1)}, u32[]{:S(2)}, u32[]{:S(2)}) collective-permute-start(bf16[2,260,128]{2,1,0:T(8,128)(2,1)S(1)} %pad_maximum_fusion.1), channel_id=1, source_target_pairs={{0,96},{32,64},{64,32},{96,0},{128,224},{160,192},{192,160},{224,1... | collective-permute-start | bytes 399368 | tf_op jit(solution)/shard_map/ppermute | solution.py:276
  35.0 7.3 %collective-permute-start.8 = (bf16[2,260,128]{2,1,0:T(8,128)(2,1)S(1)}, bf16[2,260,128]{2,1,0:T(8,128)(2,1)S(1)}, u32[]{:S(2)}, u32[]{:S(2)}) collective-permute-start(bf16[2,260,128]{2,1,0:T(8,128)(2,1)S(1)} %pad_maximum_fusion), channel_id=1, source_target_pairs={{0,64},{32,96},{64,0},{96,32},{128,192},{160,224},{192,128},{224,1... | collective-permute-start | bytes 399368 | tf_op jit(solution)/shard_map/ppermute | solution.py:276
  42.5 5.9 %collective-permute-start.11 = (bf16[1,260,128]{2,1,0:T(8,128)(2,1)S(1)}, bf16[1,260,128]{2,1,0:T(8,128)(2,1)S(1)}, u32[]{:S(2)}, u32[]{:S(2)}) collective-permute-start(bf16[1,260,128]{2,1,0:T(8,128)(2,1)S(1)} %pad_maximum_fusion.4), channel_id=1, source_target_pairs={{0,128},{32,160},{64,192},{96,224},{128,0},{160,32},{192,64},{224,... | collective-permute-start | bytes 199688 | tf_op jit(solution)/shard_map/ppermute | solution.py:282
